TPU v7x, 512 devices: a whole 4x8x8 slice. The times are simulated.
512 devices in a mesh: region: 16 (over y, core), group: 32 (over z, x).
Axes of the slice: x: 4, y: 8, z: 8, core: 2. Of those that a mesh axis runs over, the one named last changes fastest.
Arguments:
- geom: float32 [4, 262144], P(None, ('region', 'group')), as said below
- density: float32 [262144], P(('region', 'group')), may hold values from 0.5 to 4
- velocity: float32 [3, 262144], P(None, ('region', 'group')), may hold values from -3 to 3
- pressure: float32 [262144], P(('region', 'group')), may hold values from 0.5 to 4
- block_live: int32 [1024], P(('region', 'group')), may hold values from 0 to 256, as said below
- pair_list: int32 [7168, 2], P(('region', 'group')), may hold values from -1 to 1023, as said below
Outputs:
- gradients: float32 [15, 262144], P(None, ('region', 'group'))
- rate: float32 [5, 262144], P(None, ('region', 'group'))
Inputs may be any that keep to these rules, and one draw needn't show every extreme that they name: `geom`: rows are x, y, z and H. Particles sit one to a site of a cubic lattice of unit spacing, each moved by at most 0.3 along each axis; block g covers a box of 4 x 8 x 8 sites; H lies between 1.6 and 2.4. `block_live`: A block's particle slots below its count are live, the others are padding. `pair_list`: block g lives on device g // 2 (devices in region-major order) in its slot g % 2. Each device's 14 rows hold pairs (a, b) of block ids with a on that device and b equal to a or a block of the same or a neighbouring region; the row (a, b) is present exactly when the row (b, a) is present on b's device; every nonempty block has the row (a, a); no pair appears twice; rows (-1, -1) are padding and follow all other rows of a device.
All inputs are finite; a program needn't handle non-finite values.
Results may differ from a plain program's by a relative error of at most 0.0003.
Values sent between devices are 32-bit elements; how exact they have to be, the bound alone decides.
A program may use at most 64 MiB of HBM per device.

v0:
```python
import jax
import jax.numpy as jnp
from jax import lax
from jax.sharding import PartitionSpec as P

BLOCK = 256
BLK_DEV = 2


adiabatic = 5.0 / 3.0
ridge_scale = 0.05


def padded(cells, sides, width):
    for axis, dim in sides:
        count = lax.axis_size(axis)
        ends = count - 1
        head = lax.slice_in_dim(cells, 0, width, axis=dim)
        tail = lax.slice_in_dim(cells, cells.shape[dim] - width, cells.shape[dim], axis=dim)
        cells = jnp.concatenate(
            [
                lax.ppermute(tail, axis, [(i, (i + 1) % count) for i in range(ends)]),
                cells,
                lax.ppermute(head, axis, [((i + 1) % count, i) for i in range(ends)]),
            ],
            axis=dim,
        )
    return cells


def kernel_weight(scaled_distance):
    remain = jnp.maximum(1.0 - scaled_distance, 0.0)
    square = remain * remain
    return square * square * (1.0 + 4.0 * scaled_distance)


def moment_tile(block_a, block_b):
    offset = block_b[0:3, None, :] - block_a[0:3, :, None]
    distance = jnp.sqrt(jnp.sum(offset * offset, axis=0))
    change = block_b[4:9, None, :] - block_a[4:9, :, None]
    seconds = jnp.stack(
        [
            offset[0] * offset[0],
            offset[1] * offset[1],
            offset[2] * offset[2],
            offset[0] * offset[1],
            offset[0] * offset[2],
            offset[1] * offset[2],
        ]
    )
    firsts = (change[:, None] * offset[None]).reshape((15,) + distance.shape)
    term_rows = jnp.concatenate(
        [jnp.ones((1,) + distance.shape, distance.dtype), seconds, firsts], axis=0
    )
    weight_a = kernel_weight(distance / block_a[3][:, None]) * block_b[9][None, :]
    return jnp.sum(term_rows * weight_a[None], axis=2)


def finish_moments(totals, radius, alive_mask):
    omega_sum = totals[0] + (1.0 - alive_mask)
    scaled = totals[1:] / omega_sum[None]
    diagonal_shift = ridge_scale * radius * radius
    matrix = [
        scaled[0] + diagonal_shift,
        scaled[1] + diagonal_shift,
        scaled[2] + diagonal_shift,
        scaled[3],
        scaled[4],
        scaled[5],
    ]
    cofactor = [
        matrix[1] * matrix[2] - matrix[5] * matrix[5],
        matrix[0] * matrix[2] - matrix[4] * matrix[4],
        matrix[0] * matrix[1] - matrix[3] * matrix[3],
        matrix[4] * matrix[5] - matrix[3] * matrix[2],
        matrix[3] * matrix[5] - matrix[4] * matrix[1],
        matrix[3] * matrix[4] - matrix[0] * matrix[5],
    ]
    determinant = matrix[0] * cofactor[0] + matrix[3] * cofactor[3] + matrix[4] * cofactor[4]
    inverse = jnp.stack(cofactor) / determinant[None]
    moment = scaled[6:21].reshape(5, 3, -1)
    gradient_rows = jnp.stack(
        [
            inverse[0] * moment[:, 0] + inverse[3] * moment[:, 1] + inverse[4] * moment[:, 2],
            inverse[3] * moment[:, 0] + inverse[1] * moment[:, 1] + inverse[5] * moment[:, 2],
            inverse[4] * moment[:, 0] + inverse[5] * moment[:, 1] + inverse[2] * moment[:, 2],
        ],
        axis=1,
    ).reshape(15, -1)
    return jnp.concatenate([inverse, gradient_rows, omega_sum[None]], axis=0)


def riemann_side(state, normal):
    density_value = jnp.exp(state[0])
    pressure_value = jnp.exp(state[4])
    motion = state[1:4]
    normal_speed = jnp.sum(motion * normal, axis=0)
    sound_speed = jnp.sqrt(adiabatic * pressure_value / density_value)
    energy = pressure_value / (adiabatic - 1.0) + 0.5 * density_value * jnp.sum(
        motion * motion, axis=0
    )
    conserved = jnp.concatenate(
        [density_value[None], density_value[None] * motion, energy[None]], axis=0
    )
    face_flux = jnp.concatenate(
        [
            (density_value * normal_speed)[None],
            (density_value * normal_speed)[None] * motion + pressure_value[None] * normal,
            ((energy + pressure_value) * normal_speed)[None],
        ],
        axis=0,
    )
    return (
        density_value,
        pressure_value,
        motion,
        normal_speed,
        sound_speed,
        energy,
        conserved,
        face_flux,
    )


def star_flux(side_values, wave_speed, middle, normal):
    (
        density_value,
        pressure_value,
        motion,
        normal_speed,
        sound_speed,
        energy,
        conserved,
        face_flux,
    ) = side_values
    mass_rate = density_value * (wave_speed - normal_speed)
    factor = mass_rate / (wave_speed - middle)
    star_state = jnp.concatenate(
        [
            factor[None],
            factor[None] * (motion + (middle - normal_speed)[None] * normal),
            (
                factor
                * (
                    energy / density_value
                    + (middle - normal_speed) * (middle + pressure_value / mass_rate)
                )
            )[None],
        ],
        axis=0,
    )
    return face_flux + wave_speed[None] * (star_state - conserved)


def riemann(left_state, right_state, normal):
    left_side = riemann_side(left_state, normal)
    right_side = riemann_side(right_state, normal)
    speed_left = jnp.minimum(left_side[3] - left_side[4], right_side[3] - right_side[4])
    speed_right = jnp.maximum(left_side[3] + left_side[4], right_side[3] + right_side[4])
    mass_left = left_side[0] * (speed_left - left_side[3])
    mass_right = right_side[0] * (speed_right - right_side[3])
    middle = (
        right_side[1] - left_side[1] + mass_left * left_side[3] - mass_right * right_side[3]
    ) / (mass_left - mass_right)
    star_left = star_flux(left_side, speed_left, middle, normal)
    star_right = star_flux(right_side, speed_right, middle, normal)
    return jnp.where(
        speed_left[None] >= 0.0,
        left_side[7],
        jnp.where(
            middle[None] >= 0.0,
            star_left,
            jnp.where(speed_right[None] > 0.0, star_right, right_side[7]),
        ),
    )


def apply_matrix(inverse, offset):
    return jnp.stack(
        [
            inverse[0] * offset[0] + inverse[3] * offset[1] + inverse[4] * offset[2],
            inverse[3] * offset[0] + inverse[1] * offset[1] + inverse[5] * offset[2],
            inverse[4] * offset[0] + inverse[5] * offset[1] + inverse[2] * offset[2],
        ]
    )


def flux_tile(block_a, extra_a, block_b, extra_b, self_flag):
    offset = block_b[0:3, None, :] - block_a[0:3, :, None]
    diagonal = jnp.eye(offset.shape[1], dtype=offset.dtype) * self_flag
    distance = jnp.sqrt(jnp.sum(offset * offset, axis=0) + diagonal)
    normal = offset / distance[None]
    weight_a = kernel_weight(distance / block_a[3][:, None]) / (extra_a[21] * extra_a[21])[:, None]
    weight_b = kernel_weight(distance / block_b[3][None, :]) / (extra_b[21] * extra_b[21])[None, :]
    face_vector = weight_a[None] * apply_matrix(extra_a[0:6, :, None], offset) + weight_b[
        None
    ] * apply_matrix(extra_b[0:6, None, :], offset)
    face_area = jnp.sqrt(jnp.sum(face_vector * face_vector, axis=0))
    grad_a = extra_a[6:21].reshape(5, 3, -1)
    grad_b = extra_b[6:21].reshape(5, 3, -1)
    slope_a = (
        grad_a[:, 0, :, None] * offset[0][None]
        + grad_a[:, 1, :, None] * offset[1][None]
        + grad_a[:, 2, :, None] * offset[2][None]
    )
    slope_b = (
        grad_b[:, 0, None, :] * offset[0][None]
        + grad_b[:, 1, None, :] * offset[1][None]
        + grad_b[:, 2, None, :] * offset[2][None]
    )
    left_state = block_a[4:9, :, None] + 0.5 * jnp.tanh(slope_a)
    right_state = block_b[4:9, None, :] - 0.5 * jnp.tanh(slope_b)
    face_flux = riemann(left_state, right_state, normal)
    pair_weight = face_area * block_a[9][:, None] * block_b[9][None, :] * (1.0 - diagonal)
    carried = face_flux * pair_weight[None]
    return -jnp.sum(carried, axis=2)


def moment_row(head_slices, tail_slices, self_flag):
    return moment_tile(head_slices[0], tail_slices[0])


def flux_row(head_slices, tail_slices, self_flag):
    return flux_tile(head_slices[0], head_slices[1], tail_slices[0], tail_slices[1], self_flag)


def collect(payload):
    beside_all = padded(payload, (("region", 1),), payload.shape[1])
    return lax.all_gather(beside_all, "group", axis=1, tiled=True)


def add_block(total_rows, part_rows, start_column):
    current = lax.dynamic_slice_in_dim(total_rows, start_column, BLOCK, 1)
    return lax.dynamic_update_slice_in_dim(total_rows, current + part_rows, start_column, 1)


def pair_sweep(pair_list, local, remote, row_tile, out_rows, locate):
    particles = local[0].shape[1]
    carry_start = jnp.zeros((out_rows, particles), jnp.float32)

    def row_step(row_index, carry):
        head_raw = pair_list[row_index, 0]
        tail_raw = pair_list[row_index, 1]
        wanted = head_raw >= 0
        head_block = jnp.maximum(head_raw, 0)
        tail_block = jnp.maximum(tail_raw, 0)
        head_start = head_block % BLK_DEV * BLOCK
        tail_start = locate(tail_block)
        head_slices = tuple(
            (lax.dynamic_slice_in_dim(array_piece, head_start, BLOCK, 1) for array_piece in local)
        )
        tail_slices = tuple(
            (lax.dynamic_slice_in_dim(array_piece, tail_start, BLOCK, 1) for array_piece in remote)
        )
        self_flag = (head_block == tail_block).astype(jnp.float32)
        row_part = jnp.where(wanted, row_tile(head_slices, tail_slices, self_flag), 0.0)
        return add_block(carry, row_part, head_start)

    return lax.fori_loop(0, pair_list.shape[0], row_step, carry_start)


def body(geom, density, velocity, pressure, block_live, pair_list):
    group_size = lax.axis_size("group")
    region_index = lax.axis_index("region")
    particles = geom.shape[1]
    block_slot = jnp.arange(particles) % BLOCK
    alive_mask = (block_slot < jnp.repeat(block_live, BLOCK)).astype(jnp.float32)
    first_rows = jnp.concatenate(
        [geom, jnp.log(density)[None], velocity, jnp.log(pressure)[None], alive_mask[None]], axis=0
    )

    def locate(block_id):
        owner = block_id // BLK_DEV
        within = block_id % BLK_DEV
        owner_region = owner // group_size
        owner_group = owner % group_size
        layer = owner_region - region_index + 1
        slot_index = owner_group * 3 + layer
        return (slot_index * BLK_DEV + within) * BLOCK

    gathered_first = collect(first_rows)
    moment_sums = pair_sweep(pair_list, (first_rows,), (gathered_first,), moment_row, 22, locate)
    extra_rows = finish_moments(moment_sums, geom[3], alive_mask)
    gathered_extra = collect(extra_rows)
    rate_rows = pair_sweep(
        pair_list, (first_rows, extra_rows), (gathered_first, gathered_extra), flux_row, 5, locate
    )
    return (extra_rows[6:21] * alive_mask[None], rate_rows)


def solution(mesh):
    return jax.shard_map(
        body,
        mesh=mesh,
        in_specs=(
            P(None, ("region", "group")),
            P(("region", "group")),
            P(None, ("region", "group")),
            P(("region", "group")),
            P(("region", "group")),
            P(("region", "group"), None),
        ),
        out_specs=(P(None, ("region", "group")), P(None, ("region", "group"))),
        check_vma=False,
    )
```

profile of v0, /device:TPU:1, one launch (start us, length us, event | category | flops | bytes accessed | tf_op | source)
XLA Modules:
  0.0 645.6 jit_solution(4785462449979237600)
XLA Ops:
  10.1 4.6 collective-permute-start
  14.7 5.5 collective-permute-start.1
  21.7 85.3 %all-gather.3.cloned.1.call-done = f32[10,49152]{1,0:T(8,128)} async-done(((f32[10,1536]{1,0:T(8,128)}), f32[10,49152]{1,0:T(8,128)}) %all-gather.3.cloned.1.call-update) | async-done | bytes 1966096 | tf_op jit(solution)/shard_map/all_gather | solution.py:229
  107.1 249.1 %while.32 = (s32[]{:T(128)}, f32[22,512]{1,0:T(8,128)S(1)}, s32[14,2]{0,1:T(2,128)}, s32[]{:T(128)}, f32[10,49152]{1,0:T(8,128)}, /*index=5*/f32[10,512]{1,0:T(8...) while((s32[]{:T(128)}, f32[22,512]{1,0:T(8,128)S(1)}, ...), condition=%wide.region_3.4_spmd, body=%wide.region_0.3_spmd.sunk | while | flops 5707323 | bytes 27153220 | solution.py:259
  107.1 1.4 constant_dynamic-slice_fusion.15
  117.4 2.2 constant_dynamic-update-slice_fusion.2
  120.6 3.5 multiply_reduce_fusion.12
  124.8 1.4 constant_dynamic-slice_fusion.15
  135.2 2.2 constant_dynamic-update-slice_fusion.2
  138.4 3.5 multiply_reduce_fusion.12
  142.6 1.4 constant_dynamic-slice_fusion.15
  152.9 2.2 constant_dynamic-update-slice_fusion.2
  156.2 3.5 multiply_reduce_fusion.12
  160.4 1.4 constant_dynamic-slice_fusion.15
  170.7 2.2 constant_dynamic-update-slice_fusion.2
  174.0 3.5 multiply_reduce_fusion.12
  178.2 1.4 constant_dynamic-slice_fusion.15
  188.5 2.2 constant_dynamic-update-slice_fusion.2
  191.8 3.5 multiply_reduce_fusion.12
  196.0 1.4 constant_dynamic-slice_fusion.15
  206.3 2.2 constant_dynamic-update-slice_fusion.2
  209.5 3.5 multiply_reduce_fusion.12
  213.8 1.4 constant_dynamic-slice_fusion.15
  224.1 2.2 constant_dynamic-update-slice_fusion.2
  227.3 3.5 multiply_reduce_fusion.12
  231.6 1.4 constant_dynamic-slice_fusion.15
  241.9 2.2 constant_dynamic-update-slice_fusion.2
  245.1 3.5 multiply_reduce_fusion.12
  249.4 1.4 constant_dynamic-slice_fusion.15
  259.7 2.2 constant_dynamic-update-slice_fusion.2
  262.9 3.5 multiply_reduce_fusion.12
  267.2 1.4 constant_dynamic-slice_fusion.15
  277.5 2.2 constant_dynamic-update-slice_fusion.2
  280.7 3.5 multiply_reduce_fusion.12
  285.0 1.4 constant_dynamic-slice_fusion.15
  295.3 2.2 constant_dynamic-update-slice_fusion.2
  298.5 3.5 multiply_reduce_fusion.12
  302.8 1.4 constant_dynamic-slice_fusion.15
  313.1 2.2 constant_dynamic-update-slice_fusion.2
  316.3 3.5 multiply_reduce_fusion.12
  320.5 1.4 constant_dynamic-slice_fusion.15
  330.9 2.2 constant_dynamic-update-slice_fusion.2
  334.1 3.5 multiply_reduce_fusion.12
  338.3 1.4 constant_dynamic-slice_fusion.15
  348.6 2.2 constant_dynamic-update-slice_fusion.2
  351.9 3.5 multiply_reduce_fusion.12
  356.5 7.8 %collective-permute-start.2 = (f32[22,512]{1,0:T(8,128)S(1)}, f32[22,512]{1,0:T(8,128)S(1)}, u32[]{:S(2)}, u32[]{:S(2)}) collective-permute-start(f32[22,512]{1,0:T(8,128)S(1)} %pad_maximum_fusion.3), channel_id=1, source_target_pairs={{0,32},{32,64},{64,96},{96,128},{128,160},{160,192},{192,224},{224... | collective-permute-start | bytes 135176 | tf_op jit(solution)/shard_map/ppermute | solution.py:22
  364.2 1.9 collective-permute-start.3
  366.2 3.5 collective-permute-done.3
  371.0 82.6 %all-gather.5.cloned.1.call-done = f32[22,49152]{1,0:T(8,128)} async-done(((f32[22,1536]{1,0:T(8,128)}), f32[22,49152]{1,0:T(8,128)}) %all-gather.5.cloned.1.call-update) | async-done | bytes 4325392 | tf_op jit(solution)/shard_map/all_gather | solution.py:229
  453.6 184.6 %while.33 = (s32[]{:T(128)}, f32[5,512]{1,0:T(8,128)S(1)}, s32[14,2]{0,1:T(2,128)}, f32[10,512]{1,0:T(8,128)S(1)}, f32[22,512]{1,0:T(8,128)S(1)}, /*index=5*/s32...) while((s32[]{:T(128)}, f32[5,512]{1,0:T(8,128)S(1)}, ...), condition=%wide.region_12.13_spmd, body=%wide.region_4.12_spmd.sunk | while | flops 27135040 | bytes 48265216 | solution.py:259
  466.8 1.4 constant_dynamic-slice_fusion.17
  480.0 1.4 constant_dynamic-slice_fusion.17
  493.1 1.4 constant_dynamic-slice_fusion.17
  506.3 1.4 constant_dynamic-slice_fusion.17
  519.5 1.4 constant_dynamic-slice_fusion.17
  532.7 1.4 constant_dynamic-slice_fusion.17
  545.9 1.4 constant_dynamic-slice_fusion.17
  559.1 1.4 constant_dynamic-slice_fusion.17
  572.3 1.4 constant_dynamic-slice_fusion.17
  585.4 1.4 constant_dynamic-slice_fusion.17
  598.6 1.4 constant_dynamic-slice_fusion.17
  611.8 1.4 constant_dynamic-slice_fusion.17
  625.0 1.4 constant_dynamic-slice_fusion.17
  (724 shorter events, 263.4 us)
Async XLA Ops:
  7.2 99.9 %all-gather.3.cloned.1.call-start = ((), (), s32[]{:S(2)}) async-start(), calls=%async_computation | async-start | bytes 3244032 | tf_op jit(solution)/shard_map/all_gather | solution.py:229
  10.1 10.1 %collective-permute-start = (f32[10,512]{1,0:T(8,128)S(1)}, f32[10,512]{1,0:T(8,128)S(1)}, u32[]{:S(2)}, u32[]{:S(2)}) collective-permute-start(f32[10,512]{1,0:T(8,128)S(1)} %concatenate.89), channel_id=1, source_target_pairs={{0,32},{32,64},{64,96},{96,128},{128,160},{160,192},{192,224},{224... | collective-permute-start | bytes 61448 | tf_op jit(solution)/shard_map/ppermute | solution.py:22
  14.7 6.3 collective-permute-start.1
  21.7 431.9 %all-gather.5.cloned.1.call-start = ((), (), s32[]{:S(2)}) async-start(), calls=%async_computation.1 | async-start | bytes 4866048 | tf_op jit(solution)/shard_map/all_gather | solution.py:229
  107.1 249.1 %copy-start.1 = (f32[4,512]{1,0:T(4,128)S(1)}, f32[4,512]{1,0:T(4,128)}, u32[]{:S(2)}) copy-start(f32[4,512]{1,0:T(4,128)} %param.10) | copy-start | bytes 24580
  356.5 9.7 %collective-permute-start.2 = (f32[22,512]{1,0:T(8,128)S(1)}, f32[22,512]{1,0:T(8,128)S(1)}, u32[]{:S(2)}, u32[]{:S(2)}) collective-permute-start(f32[22,512]{1,0:T(8,128)S(1)} %pad_maximum_fusion.3), channel_id=1, source_target_pairs={{0,32},{32,64},{64,96},{96,128},{128,160},{160,192},{192,224},{224... | collective-permute-start | bytes 135176 | tf_op jit(solution)/shard_map/ppermute | solution.py:22
  364.2 5.4 collective-permute-start.3
  638.2 0.6 copy-start
Sparse Core Ops, SparseCore 0:
  21.8 85.2 all-gather.2
  370.5 83.0 all-gather.4
where the time goes:
time: 655 us; the launch traced here: 646 us
  other arithmetic  216 us (33%)
  waiting for transfers between devices  172 us (26%)
  local copies, waits for them, and re-layouts  165 us (25%)
  loops' own time  58.8 us (9%)
  starting transfers between devices  19.8 us (3%)
  between operations  14.2 us (2%)
    all_gather x2, waiting for transfers between devices, collect(): return lax.all_gather(beside_all, 'group', axis=1, tiled=True)  168 us
    while x84, other arithmetic  61.5 us
    another operation x2, loops' own time, pair_sweep(): return lax.fori_loop(0, pair_list.shape[0], row_step, carry_start)  58.8 us
    reduce_sum x14, other arithmetic, moment_tile(): return jnp.sum(term_rows * weight_a[None], axis=2)  49.2 us
    dynamic_slice x28, local copies, waits for them, and re-layouts, row_step(): tail_raw = pair_list[row_index, 1]  39.5 us
    concatenate x14, local copies, waits for them, and re-layouts, moment_tile(): jnp.concatenate([jnp.ones((1,) + distance.shape, distance.dtype), seconds...  30.7 us
    reduce_sum x14, other arithmetic, flux_tile(): return -jnp.sum(carried, axis=2)  16.1 us
    slice x14, other arithmetic, apply_matrix(): inverse[0] * offset[0] + inverse[3] * offset[1] + inverse[4] * offset[2]  14.5 us
  transfers between devices with their start and end apart: 6, of which 4 were waited for; matrix products, arithmetic and copies ran while one was open for 0% of the time, Pallas kernels for 0%

commit v1 on v0

v1 whole, which is shorter than its diff:
```python
import functools

import jax
import jax.numpy as jnp
from jax import lax
from jax.experimental import pallas as pl
from jax.experimental.pallas import tpu as pltpu
from jax.sharding import PartitionSpec as P

BLOCK = 256
LIST = 14
LAYERS = 3
F32 = jnp.float32
BF16 = jnp.bfloat16
ridge_scale = 0.05
gamma = 5.0 / 3.0
HEAD, TAIL, CODE = 64, 78, 92
SELF = 13


def iota(shape, dim):
    return lax.broadcasted_iota(jnp.int32, shape, dim)


def split3(value):
    high = value.astype(BF16)
    rest = value - high.astype(F32)
    middle = rest.astype(BF16)
    low = (rest - middle.astype(F32)).astype(BF16)
    return high, middle, low


def prepare(geom, density, velocity, pressure, live, pair, chunk, place):
    lanes = iota((1, 128), 1)
    total = jnp.zeros((40, 128), F32)
    line = jnp.zeros((1, 128), F32)
    heads = pair[:, 0:1].astype(F32)
    tails = pair[:, 1:2].astype(F32)
    row_lane = iota((LIST, 128), 1) - iota((LIST, 128), 0)
    listed = jnp.where(row_lane == HEAD, heads, 0.0) + jnp.where(row_lane == TAIL, tails, 0.0)
    line = line + jnp.sum(listed, axis=0, keepdims=True)
    for s in range(2):
        at = slice(s * BLOCK, (s + 1) * BLOCK)
        corner = geom[:, at]
        columns = jnp.concatenate([corner, corner], axis=0).T
        cells = []
        for k, count in ((0, 64), (1, 32), (2, 32)):
            smaller = columns[:, k : k + 1] < corner[k : k + 1, :]
            rank = jnp.sum(jnp.where(smaller, 1.0, 0.0), axis=0, keepdims=True)
            cells.append(jnp.floor(rank * (1.0 / count)).astype(jnp.int32))
            low = jnp.min(corner[k : k + 1, :], axis=1, keepdims=True)
            line = line + jnp.where(lanes == CODE + 3 * s + k, low, 0.0)
        lane = cells[0] * 8 + cells[2]
        alive = iota((1, BLOCK), 1) < live[s]
        rows = [corner[0:1], corner[1:2], corner[2:3], jnp.log(density[:, at])]
        rows += [velocity[k : k + 1, at] for k in range(3)]
        rows += [jnp.log(pressure[:, at]), jnp.where(alive, corner[3:4], 0.0)]
        here = iota((8, BLOCK), 0) == cells[1]
        spread = [jnp.where(here, row, 0.0) for row in rows] + [jnp.zeros((8, BLOCK), F32)]
        for par in range(2):
            target = jnp.where(iota((128, BLOCK), 0) == lane + (par * 64 + s * 32), 1.0, 0.0)
            target = target.astype(BF16)
            for part in split3(jnp.concatenate(spread[par::2], axis=0)):
                total = total + lax.dot_general(
                    part, target, (((1,), (1,)), ((), ())), preferred_element_type=F32
                )
        place[0:1, at] = cells[1].astype(F32)
        place[1:2, at] = (cells[0] * 16 + cells[2] + 8 * s).astype(F32)
        place[2:3, at] = jnp.where(alive, 1.0, 0.0)
    chunk[...] = total + jnp.where(iota((40, 128), 0) == 32, line, 0.0)


def prepare_call(geom, density, velocity, pressure, live, pair):
    vmem = pl.BlockSpec(memory_space=pltpu.VMEM)
    smem = pl.BlockSpec(memory_space=pltpu.SMEM)
    return pl.pallas_call(
        prepare,
        out_shape=(jax.ShapeDtypeStruct((40, 128), F32), jax.ShapeDtypeStruct((8, 512), F32)),
        in_specs=[vmem, vmem, vmem, vmem, smem, vmem],
        out_specs=(vmem, vmem),
        name="site_order",
    )(geom, density[None], velocity, pressure[None], live, pair)


def make_lines(rows, own, region):
    lanes = iota(rows.shape, 1)
    kind = (lanes - CODE) % 3
    scale = jnp.where(kind == 0, 0.25, 0.125)
    weight = jnp.where(kind == 0, 1024.0, jnp.where(kind == 1, 32.0, 1.0))
    origin = jnp.where(lanes[0:1] >= CODE + 3, jnp.roll(own, 3, axis=1), own)
    steps = jnp.floor((rows - origin) * scale + 0.5) * weight
    steps = steps + jnp.roll(steps, -1, axis=1) + jnp.roll(steps, -2, axis=1)
    whole = jnp.where(lanes < CODE, rows, steps).astype(jnp.int32)
    return whole


def locate(block, region):
    owner = block // 2
    layer = owner // 32 - region + 1
    return layer, (owner % 32) * LAYERS + layer, block % 2


def direction(step):
    u = step + 1057
    a, b, c = u >> 10, (u >> 5) & 31, u & 31
    valid = (u >= 0) & (a <= 2) & (b <= 2) & (c <= 2)
    return valid, a * 9 + b * 3 + c


def fill_tables(lines, region, own, source, used, faces, face_used):
    def clear(k, _):
        source[k] = -1
        return _

    lax.fori_loop(0, 27 * 16, clear, 0, unroll=16)

    def clear_dir(k, _):
        used[k] = 0
        face_used[k] = 0
        faces[k] = -1
        faces[27 + k] = -1
        return _

    lax.fori_loop(0, 27, clear_dir, 0, unroll=9)

    def slot(p, _):
        head = lines[own, HEAD + p]
        tail = lines[own, TAIL + p]

        @pl.when(head >= 0)
        def _row():
            _, at, s = locate(tail, region)
            place = lines[at, CODE + 3 * s]
            home = lines[own, CODE + 3 * (head % 2)]
            valid, way = direction(place - home)

            @pl.when(valid)
            def _face():
                faces[(head % 2) * 27 + way] = p
                face_used[way] = 1

            def entry(k, _):
                @pl.when(lines[at, HEAD + k] == tail)
                def _listed():
                    layer, there, t = locate(lines[at, TAIL + k], region)
                    near = (layer >= 0) & (layer < LAYERS)
                    there = jnp.where(near, there, 0)
                    fits, towards = direction(lines[there, CODE + 3 * t] - place)

                    @pl.when(fits & near)
                    def _set():
                        source[towards * 16 + p] = there * 2 + t
                        used[towards] = 1

                return _

            lax.fori_loop(0, LIST, entry, 0)

        return _

    lax.fori_loop(0, LIST, slot, 0)


def gather_sites(chunks, source, used, near):
    group = iota((8, 128), 1) // 8

    def one_way(way, _):
        @pl.when(used[way] > 0)
        def _present():
            froms = [source[way * 16 + p] for p in range(LIST)]
            wanted = [jnp.where(f >= 0, p, -1) for p, f in enumerate(froms)]
            froms = [jnp.maximum(f, 0) for f in froms]

            def one_tile(t, _):
                sums = [jnp.zeros((8, 128), F32) for _k in range(8)]
                for p in range(LIST):
                    tile = chunks[froms[p] // 2, pl.ds(pl.multiple_of(t * 8, 8), 8), :]
                    tile = pltpu.roll(tile, (froms[p] % 2) * 96 + p * 8, 1)
                    mask = group == wanted[p]
                    for k in range(8):
                        moved = pltpu.roll(tile, (128 - 64 * (k // 4) - 8 * (k % 4)) % 128, 1)
                        sums[k] = jnp.where(mask, moved, sums[k])
                for k in range(8):
                    near[way, 2 * t + k // 4, k % 4] = sums[k]
                return _

            lax.fori_loop(0, 5, one_tile, 0)
            for x in range(4):
                radius = near[way, 8, x]
                near[way, 9, x] = radius
                near[way, 8, x] = jnp.where(radius > 0.0, 1.0, 0.0)

        @pl.when(used[way] == 0)
        def _absent():
            near[way] = jnp.zeros((10, 4, 8, 128), F32)

        return _

    lax.fori_loop(0, 27, one_way, 0)


def shifted(base, below, above, z, dz):
    if dz == 0:
        return base
    inside = pltpu.roll(base, (-dz) % 128, 1)
    if dz > 0:
        return jnp.where(z + dz < 8, inside, pltpu.roll(above, 8 - dz, 1))
    return jnp.where(z + dz >= 0, inside, pltpu.roll(below, 128 - 8 - dz, 1))


def shift_sites(near, halo):
    z = iota((8, 128), 1) % 8

    def one_row(row, _):
        for xe in range(8):
            sx, x = (0, xe + 2) if xe < 2 else (1, xe - 2) if xe < 6 else (2, xe - 6)
            for sy in range(3):
                base, below, above = [near[sx * 9 + sy * 3 + sz, row, x] for sz in (1, 0, 2)]
                for dz in range(-2, 3):
                    halo[dz + 2, row, xe, 8 * sy : 8 * sy + 8, :] = shifted(
                        base, below, above, z, dz
                    )
        return _

    lax.fori_loop(0, 9, one_row, 0)


def moments(near, halo, fields):
    def one_plane(x, _):
        xi, yi, zi = [near[SELF, k, x] for k in range(3)]
        qi = [near[SELF, 3 + k, x] for k in range(5)]
        alive, radius = near[SELF, 8, x], near[SELF, 9, x]
        radius = jnp.where(radius > 0.0, radius, 1.0)
        inverse_radius = 1.0 / radius

        def step(n, sums):
            dz = n // 5
            xe = n % 5 + x
            sums = list(sums)
            for dy in range(-2, 3):
                near_j = [halo[dz, k, xe, 8 + dy : 16 + dy, :] for k in range(9)]
                ox, oy, oz = near_j[0] - xi, near_j[1] - yi, near_j[2] - zi
                square = ox * ox + oy * oy + oz * oz
                scaled = square * lax.rsqrt(jnp.maximum(square, 1e-12)) * inverse_radius
                remain = jnp.maximum(1.0 - scaled, 0.0)
                remain = remain * remain
                w = remain * remain * (1.0 + 4.0 * scaled) * near_j[8]
                wx, wy, wz = w * ox, w * oy, w * oz
                terms = [w, wx * ox, wy * oy, wz * oz, wx * oy, wx * oz, wy * oz]
                for k in range(5):
                    change = near_j[3 + k] - qi[k]
                    terms += [wx * change, wy * change, wz * change]
                sums = [a + b for a, b in zip(sums, terms)]
            return tuple(sums)

        zero = jnp.zeros((8, 128), F32)
        sums = lax.fori_loop(0, 25, step, (zero,) * 22)
        omega = sums[0] + (1.0 - alive)
        per = 1.0 / omega
        shift = ridge_scale * radius * radius
        m = [sums[1 + k] * per for k in range(6)]
        m[0], m[1], m[2] = m[0] + shift, m[1] + shift, m[2] + shift
        c = [
            m[1] * m[2] - m[5] * m[5],
            m[0] * m[2] - m[4] * m[4],
            m[0] * m[1] - m[3] * m[3],
            m[4] * m[5] - m[3] * m[2],
            m[3] * m[5] - m[4] * m[1],
            m[3] * m[4] - m[0] * m[5],
        ]
        over = 1.0 / (m[0] * c[0] + m[3] * c[3] + m[4] * c[4])
        b = [v * over for v in c]
        rows = [xi, yi, zi] + qi + [near[SELF, 9, x]]
        square = per * per
        rows += [v * square for v in b]
        for k in range(5):
            f = [sums[7 + 3 * k + a] * per for a in range(3)]
            rows.append(b[0] * f[0] + b[3] * f[1] + b[4] * f[2])
            rows.append(b[3] * f[0] + b[1] * f[1] + b[5] * f[2])
            rows.append(b[4] * f[0] + b[5] * f[1] + b[2] * f[2])
        for k in range(10):
            pair = jnp.concatenate(rows[3 * k : 3 * k + 3], axis=0)
            for n, part in enumerate(split3(pair)):
                fields[x, n, 24 * k : 24 * k + 24, :] = part.astype(F32)
        return _

    lax.fori_loop(0, 4, one_plane, 0)


def gather_fields(fields, faces, face_used, around):
    lanes = iota((1, 128), 1)
    z = lanes % 8
    sources = iota((128, 128), 0)

    def one_way(n, _):
        sz = n // 3
        sy = n % 3
        any_used = face_used[sy * 3 + sz] + face_used[9 + sy * 3 + sz] + face_used[18 + sy * 3 + sz]

        @pl.when(any_used > 0)
        def _present():
            total = jnp.zeros((240, 128), F32)
            for x in range(4):
                wanted = jnp.full((1, 128), -1, jnp.int32)
                for sx, xe in ((1, x + 2), (2, x + 6) if x < 2 else (0, x - 2)):
                    for s in range(2):
                        p = faces[s * 27 + sx * 9 + sy * 3 + sz]
                        lane = jnp.where(p >= 0, p * 8 + z, -1)
                        wanted = jnp.where(lanes // 8 == xe * 2 + s, lane, wanted)
                hot = jnp.where(sources == wanted, 1.0, 0.0).astype(BF16)
                for k in range(3):
                    total = total + jnp.dot(
                        fields[x, k].astype(BF16), hot, preferred_element_type=F32
                    )
            around[n] = total

        @pl.when(any_used == 0)
        def _absent():
            around[n] = jnp.zeros((240, 128), F32)

        return _

    lax.fori_loop(0, 9, one_way, 0)


def shift_fields(around, wide):
    lanes = iota((8, 128), 1)
    z = lanes % 8
    left = lanes < 64

    def one_row(row, _):
        at = pl.ds(pl.multiple_of(row * 8, 8), 8)
        for sy in range(3):
            base, below, above = [around[sz * 3 + sy, at, :] for sz in (1, 0, 2)]
            for dz in range(-2, 3):
                far = shifted(base, below, above, z, dz)
                rows = slice(8 * sy, 8 * sy + 8)
                wide[dz + 2, 0, row, rows, :] = far
                for k, step in ((1, 16), (2, 32)):
                    both = jnp.where(left, pltpu.roll(far, 128 - step, 1), pltpu.roll(far, step, 1))
                    wide[dz + 2, k, row, rows, :] = both
        return _

    lax.fori_loop(0, 30, one_row, 0)


def weight(scaled):
    remain = jnp.maximum(1.0 - scaled, 0.0)
    remain = remain * remain
    return remain * remain * (1.0 + 4.0 * scaled)


def side(state, n):
    density, pressure = jnp.exp(state[0]), jnp.exp(state[4])
    v = state[1:4]
    speed = v[0] * n[0] + v[1] * n[1] + v[2] * n[2]
    sound = jnp.exp(0.5 * (state[4] - state[0])) * (gamma**0.5)
    return density, pressure, v[0], v[1], v[2], speed, sound


def face(near, far):
    o = [far(k) - near(k) for k in range(3)]
    square = jnp.maximum(o[0] * o[0] + o[1] * o[1] + o[2] * o[2], 1e-12)
    inverse = lax.rsqrt(square)
    distance = square * inverse
    n = [v * inverse for v in o]
    hi, hj = near(8), far(8)
    live = jnp.minimum(hi, hj) > 0.0
    wi = weight(distance * (1.0 / jnp.where(hi > 0.0, hi, 1.0)))
    wj = weight(distance * (1.0 / jnp.where(hj > 0.0, hj, 1.0)))
    c = [wi * near(9 + k) + wj * far(9 + k) for k in range(6)]
    a = [
        c[0] * o[0] + c[3] * o[1] + c[4] * o[2],
        c[3] * o[0] + c[1] * o[1] + c[5] * o[2],
        c[4] * o[0] + c[5] * o[1] + c[2] * o[2],
    ]
    area = a[0] * a[0] + a[1] * a[1] + a[2] * a[2]
    area = jnp.where(live, jnp.sqrt(area), 0.0)
    left, right = [], []
    for k in range(5):
        gi = near(15 + 3 * k) * o[0] + near(16 + 3 * k) * o[1] + near(17 + 3 * k) * o[2]
        gj = far(15 + 3 * k) * o[0] + far(16 + 3 * k) * o[1] + far(17 + 3 * k) * o[2]
        left.append(near(3 + k) + 0.5 * jnp.tanh(gi))
        right.append(far(3 + k) - 0.5 * jnp.tanh(gj))
    sl, sr = side(left, n), side(right, n)
    slow = jnp.minimum(sl[5] - sl[6], sr[5] - sr[6])
    fast = jnp.maximum(sl[5] + sl[6], sr[5] + sr[6])
    ml, mr = sl[0] * (slow - sl[5]), sr[0] * (fast - sr[5])
    middle = (sr[1] - sl[1] + ml * sl[5] - mr * sr[5]) / (ml - mr)
    from_left = (slow >= 0.0) | (middle >= 0.0)
    density, pressure, v0, v1, v2, speed, _ = [
        jnp.where(from_left, p, q) for p, q in zip(sl, sr)
    ]
    mass, wave = jnp.where(from_left, ml, mr), jnp.where(from_left, slow, fast)
    star = jnp.where(from_left, -slow, fast) > 0.0
    kinetic = 0.5 * (v0 * v0 + v1 * v1 + v2 * v2)
    energy = pressure * (1.0 / (gamma - 1.0)) + density * kinetic
    push = jnp.where(star, wave * mass / (wave - middle), 0.0)
    rest = speed - jnp.where(star, wave, 0.0)
    lift = middle - speed
    flow = density * rest + push
    press = pressure + push * lift
    heat = energy * rest + pressure * speed
    heat = heat + push * (energy / density + lift * (middle + pressure / mass))
    terms = [flow, v0 * flow + press * n[0], v1 * flow + press * n[1], v2 * flow + press * n[2]]
    return [jnp.where(live, t * area, 0.0) for t in terms + [heat]]


def fluxes(wide):
    half = iota((8, 128), 1) < 64

    def near(row):
        return wide[2, 2, row, 8:16, :]

    def add(sums, far):
        return tuple(a + b for a, b in zip(sums, face(near, far)))

    def step(dz, sums):
        for k in range(2):
            for dy in range(-2, 3):
                sums = add(sums, lambda row: wide[dz, k, row, 8 + dy : 16 + dy, :])
        for d in (-2, 1):
            sums = add(
                sums,
                lambda row: jnp.where(
                    half, wide[dz, 2, row, 8 + d : 16 + d, :], wide[dz, 2, row, 9 + d : 17 + d, :]
                ),
            )
        return sums

    sums = lax.fori_loop(0, 5, step, (jnp.zeros((8, 128), F32),) * 5)
    for d in (0, 1):
        sums = add(
            sums, lambda row: jnp.where(half, wide[d, 2, row, 8:16, :], wide[4 - d, 2, row, 8:16, :])
        )
    return [-(v + pltpu.roll(v, 64, 1)) for v in sums]


def sweep(
    lines, chunks, place, gradients, rate, source, used, faces, face_used, near, halo, fields,
    around, wide,
):
    region, own = lines[0, 126], lines[0, 127]
    fill_tables(lines, region, own, source, used, faces, face_used)
    gather_sites(chunks, source, used, near)
    shift_sites(near, halo)
    moments(near, halo, fields)
    gather_fields(fields, faces, face_used, around)
    shift_fields(around, wide)
    rates = fluxes(wide)
    rows = [wide[2, 2, 15 + k, 8:16, :] for k in range(15)] + rates
    found = jnp.concatenate(rows, axis=0)
    lane = place[1:2, :].astype(jnp.int32)
    hot = jnp.where(iota((128, 512), 0) == lane, 1.0, 0.0).astype(BF16)
    total = jnp.zeros((160, 512), F32)
    for part in split3(found):
        total = total + jnp.dot(part, hot, preferred_element_type=F32)
    here = (iota((8, 512), 0) == place[0:1, :].astype(jnp.int32)) & (place[2:3, :] > 0.0)
    for k in range(20):
        row = jnp.sum(jnp.where(here, total[8 * k : 8 * k + 8], 0.0), axis=0, keepdims=True)
        if k < 15:
            gradients[k : k + 1, :] = row
        else:
            rate[k - 15 : k - 14, :] = row


def sweep_call(lines, chunks, place):
    vmem = pl.BlockSpec(memory_space=pltpu.VMEM)
    smem = pl.BlockSpec(memory_space=pltpu.SMEM)
    return pl.pallas_call(
        sweep,
        out_shape=(jax.ShapeDtypeStruct((15, 512), F32), jax.ShapeDtypeStruct((5, 512), F32)),
        in_specs=[smem, vmem, vmem],
        out_specs=(vmem, vmem),
        scratch_shapes=[
            pltpu.SMEM((27 * 16,), jnp.int32),
            pltpu.SMEM((27,), jnp.int32),
            pltpu.SMEM((54,), jnp.int32),
            pltpu.SMEM((27,), jnp.int32),
            pltpu.VMEM((27, 10, 4, 8, 128), F32),
            pltpu.VMEM((5, 9, 8, 24, 128), F32),
            pltpu.VMEM((4, 3, 240, 128), F32),
            pltpu.VMEM((9, 240, 128), F32),
            pltpu.VMEM((5, 3, 30, 24, 128), F32),
        ],
        compiler_params=pltpu.CompilerParams(vmem_limit_bytes=48 * 1024 * 1024),
        name="sweep",
    )(lines, chunks, place)


def beside(chunk):
    count = lax.axis_size("region")
    up = [(i, i + 1) for i in range(count - 1)]
    down = [(i + 1, i) for i in range(count - 1)]
    below, above = lax.ppermute(chunk, "region", up), lax.ppermute(chunk, "region", down)
    return jnp.stack([below, chunk, above])


def body(geom, density, velocity, pressure, block_live, pair_list):
    chunk, place = prepare_call(geom, density, velocity, pressure, block_live, pair_list)
    chunks = lax.all_gather(beside(chunk), "group", axis=0, tiled=True)
    region = lax.axis_index("region")
    own = lax.axis_index("group") * LAYERS + 1
    lines = make_lines(chunks[:, 32, :], chunk[32:33, :], region)
    tag = jnp.where(iota((1, 128), 1) == 126, region, own)
    lines = jnp.where(iota(lines.shape, 1) >= 126, tag, lines)
    return sweep_call(lines, chunks, place)


def solution(mesh):
    both = ("region", "group")
    return jax.shard_map(
        body,
        mesh=mesh,
        in_specs=(P(None, both), P(both), P(None, both), P(both), P(both), P(both, None)),
        out_specs=(P(None, both), P(None, both)),
        check_vma=False,
    )
```

time: 655 us -> 163 us (0.25)
  the two profiles are of different devices: /device:TPU:1 before, /device:TPU:24 now
where the time goes in v1:
time: 163 us
  waiting for transfers between devices  90 us (55%)
  Pallas kernels  45.9 us (28%)
  between operations  14.1 us (9%)
  local copies, waits for them, and re-layouts  6.23 us (4%)
  starting transfers between devices  4.35 us (3%)
  other arithmetic  2.29 us (1%)
    all_gather x1, waiting for transfers between devices, body(): chunks = lax.all_gather(beside(chunk), 'group', axis=0, tiled=True)  87.1 us
    pallas_call x1, Pallas kernels, sweep_call(): pl.pallas_call(sweep, out_shape=(jax.ShapeDtypeStruct((15, 512), F32), ja...  43.7 us
    unnamed x5, local copies, waits for them, and re-layouts  3.61 us
  transfers between devices with their start and end apart: 3, of which 2 were waited for; matrix products, arithmetic and copies ran while one was open for 1% of the time, Pallas kernels for 0%

profile of v1, /device:TPU:24, one launch (start us, length us, event | category | flops | bytes accessed | tf_op | source)
XLA Modules:
  0.0 162.8 jit_solution(14927801614364964620)
XLA Ops:
  7.2 0.0 all-gather.2.cloned.1.call-start
  7.2 1.4 copy.9.pair
  8.6 2.2 %site_order.1 = (f32[40,128]{1,0:T(8,128)}, f32[8,512]{1,0:T(8,128)}) custom-call(f32[4,512]{1,0:T(4,128)} %geom.1, f32[1,512]{1,0:T(1,128)} %bitcast.19, f32[3,512]{1,0:T(4,128)} %velocity.1, f32[1,512]{1,0:T(1,128)} %bitcast.20, s32[2]{0:T(128)} %live.1, s32[14,2]{1,0:T(8,128)} %copy.9.pair), custom_call_target="tpu_custom_call" | custom-call | tf_op jit(solution)/shard_map/site_order/pallas_call | solution.py:76
  10.8 1.9 %collective-permute-start.1 = (f32[40,128]{1,0:T(8,128)}, f32[40,128]{1,0:T(8,128)S(1)}, u32[]{:S(2)}, u32[]{:S(2)}) collective-permute-start(f32[40,128]{1,0:T(8,128)} %get-tuple-element.4), channel_id=1, source_target_pairs={{32,0},{64,32},{96,64},{128,96},{160,128},{192,160},{224,192},{256... | collective-permute-start | bytes 61448 | tf_op jit(solution)/shard_map/ppermute | solution.py:495
  12.7 2.4 %collective-permute-start = (f32[40,128]{1,0:T(8,128)}, f32[40,128]{1,0:T(8,128)S(1)}, u32[]{:S(2)}, u32[]{:S(2)}) collective-permute-start(f32[40,128]{1,0:T(8,128)} %get-tuple-element.4), channel_id=1, source_target_pairs={{0,32},{32,64},{64,96},{96,128},{128,160},{160,192},{192,224},{224... | collective-permute-start | bytes 61448 | tf_op jit(solution)/shard_map/ppermute | solution.py:495
  15.1 0.0 collective-permute-done.1
  15.1 2.9 %collective-permute-done = f32[40,128]{1,0:T(8,128)S(1)} collective-permute-done((f32[40,128]{1,0:T(8,128)}, f32[40,128]{1,0:T(8,128)S(1)}, u32[]{:S(2)}, u32[]{:S(2)}) %collective-permute-start) | collective-permute-done | bytes 20512 | tf_op jit(solution)/shard_map/ppermute | solution.py:495
  18.0 1.4 pad_maximum_fusion
  19.4 0.0 all-gather.2.cloned.1.call-update
  19.4 0.7 slice.35
  20.1 0.8 slice.34
  20.9 0.8 fusion.10
  21.7 87.1 %all-gather.2.cloned.1.call-done.chunks = f32[96,40,128]{2,1,0:T(8,128)} async-done(((f32[3,40,128]{2,1,0:T(8,128)}), f32[96,40,128]{2,1,0:T(8,128)}) %all-gather.2.cloned.1.call-update) | async-done | bytes 1966096 | tf_op jit(solution)/shard_map/all_gather | solution.py:501
  108.7 1.0 slice.41
  109.8 0.1 slice.44
  109.9 0.1 slice.42
  109.9 0.1 fusion.9.lines
  110.1 0.0 copy-start
  110.1 1.5 copy-done
  111.6 0.0 copy-start.1
  111.6 0.7 copy-done.1
  112.3 43.7 %sweep.1 = (f32[15,512]{1,0:T(8,128)}, f32[5,512]{1,0:T(8,128)}) custom-call(s32[96,128]{1,0:T(8,128)S(1)} %fusion.9.lines, f32[96,40,128]{2,1,0:T(8,128)S(1)} %copy-done, f32[8,512]{1,0:T(8,128)S(1)} %copy-done.1), custom_call_target="tpu_custom_call" | custom-call | tf_op jit(solution)/shard_map/sweep/pallas_call | solution.py:470
  (5 shorter events, 0.1 us)
Async XLA Ops:
  7.2 101.6 %all-gather.2.cloned.1.call-start = ((), (), s32[]{:S(2)}) async-start(), calls=%async_computation | async-start | bytes 2027520 | tf_op jit(solution)/shard_map/all_gather | solution.py:501
  10.8 4.3 %collective-permute-start.1 = (f32[40,128]{1,0:T(8,128)}, f32[40,128]{1,0:T(8,128)S(1)}, u32[]{:S(2)}, u32[]{:S(2)}) collective-permute-start(f32[40,128]{1,0:T(8,128)} %get-tuple-element.4), channel_id=1, source_target_pairs={{32,0},{64,32},{96,64},{128,96},{160,128},{192,160},{224,192},{256... | collective-permute-start | bytes 61448 | tf_op jit(solution)/shard_map/ppermute | solution.py:495
  12.7 5.3 %collective-permute-start = (f32[40,128]{1,0:T(8,128)}, f32[40,128]{1,0:T(8,128)S(1)}, u32[]{:S(2)}, u32[]{:S(2)}) collective-permute-start(f32[40,128]{1,0:T(8,128)} %get-tuple-element.4), channel_id=1, source_target_pairs={{0,32},{32,64},{64,96},{96,128},{128,160},{160,192},{192,224},{224... | collective-permute-start | bytes 61448 | tf_op jit(solution)/shard_map/ppermute | solution.py:495
  110.1 1.5 copy-start
  111.6 0.7 copy-start.1
Sparse Core Ops, SparseCore 0:
  19.5 89.1 all-gather.1

commit v2 on v1

--- a/solution.py
+++ b/solution.py
@@ -14,7 +14,8 @@
 BF16 = jnp.bfloat16
 ridge_scale = 0.05
 gamma = 5.0 / 3.0
-HEAD, TAIL, CODE = 64, 78, 92
+HEAD, TAIL, CORNER = 64, 78, 92
+MESH = pl.DeviceIdType.MESH
 SELF = 13
 
 
@@ -30,15 +31,13 @@
     return high, middle, low
 
 
-def prepare(geom, density, velocity, pressure, live, pair, chunk, place):
+def prepare(geom, density, velocity, pressure, live, pair, line, place):
     lanes = iota((1, 128), 1)
     total = jnp.zeros((40, 128), F32)
-    line = jnp.zeros((1, 128), F32)
-    heads = pair[:, 0:1].astype(F32)
-    tails = pair[:, 1:2].astype(F32)
-    row_lane = iota((LIST, 128), 1) - iota((LIST, 128), 0)
-    listed = jnp.where(row_lane == HEAD, heads, 0.0) + jnp.where(row_lane == TAIL, tails, 0.0)
-    line = line + jnp.sum(listed, axis=0, keepdims=True)
+    line[...] = jnp.zeros((8, 128), F32)
+    line[0:1, HEAD : HEAD + LIST] = pair[0:1, :].astype(F32)
+    line[0:1, TAIL : TAIL + LIST] = pair[1:2, :].astype(F32)
+    listed = line[0:1, :]
     for s in range(2):
         at = slice(s * BLOCK, (s + 1) * BLOCK)
         corner = geom[:, at]
@@ -49,7 +48,7 @@
             rank = jnp.sum(jnp.where(smaller, 1.0, 0.0), axis=0, keepdims=True)
             cells.append(jnp.floor(rank * (1.0 / count)).astype(jnp.int32))
             low = jnp.min(corner[k : k + 1, :], axis=1, keepdims=True)
-            line = line + jnp.where(lanes == CODE + 3 * s + k, low, 0.0)
+            listed = listed + jnp.where(lanes == CORNER + 3 * s + k, low, 0.0)
         lane = cells[0] * 8 + cells[2]
         alive = iota((1, BLOCK), 1) < live[s]
         rows = [corner[0:1], corner[1:2], corner[2:3], jnp.log(density[:, at])]
@@ -67,37 +66,157 @@
         place[0:1, at] = cells[1].astype(F32)
         place[1:2, at] = (cells[0] * 16 + cells[2] + 8 * s).astype(F32)
         place[2:3, at] = jnp.where(alive, 1.0, 0.0)
-    chunk[...] = total + jnp.where(iota((40, 128), 0) == 32, line, 0.0)
-
-
-def prepare_call(geom, density, velocity, pressure, live, pair):
+    return total + jnp.where(iota((40, 128), 0) == 32, listed, 0.0)
+
+
+def read_lists(chunks, lists, region, group):
+    lanes = iota((32, 128), 1)
+    kind = (lanes - CORNER) % 3
+    scale = jnp.where(kind == 0, 0.25, 0.125)
+    weight = jnp.where(kind == 0, 1024.0, jnp.where(kind == 1, 32.0, 1.0))
+    own = chunks[32 + group, 32:33, :]
+    own = jnp.where(lanes[0:1] >= CORNER + 3, pltpu.roll(own, 3, 1), own)
+    whole = jnp.where(lanes == 96, region, group)
+    for layer in range(LAYERS):
+        rows = chunks[32 * layer : 32 * layer + 32, 32, :]
+        steps = jnp.floor((rows - own) * scale + 0.5) * weight
+        steps = steps + pltpu.roll(steps, 127, 1) + pltpu.roll(steps, 126, 1)
+        rows = pltpu.roll(jnp.where(lanes < CORNER, rows, steps), 64 + 32 * layer, 1)
+        whole = jnp.where(lanes // 32 == layer, rows.astype(jnp.int32), whole)
+    lists[...] = whole
+
+
+def exchange(
+    geom, density, velocity, pressure, live, pair, chunks, place, lists, line,
+    x_send, x_recv, z_send, z_recv, r_send, r_recv,
+):
+    region, group = lax.axis_index("region"), lax.axis_index("group")
+    z, x = group // 4, group % 4
+
+    def column(step):
+        return (region, z * 4 + (x + step) % 4)
+
+    def plane(step):
+        return (region, (z + 8 + step) % 8 * 4 + x)
+
+    def slab(step):
+        return ((region + 16 + step) % 16, group)
+
+    partners = [column(k) for k in (1, 2, 3)] + [plane(1), plane(-1), slab(1), slab(-1)]
+    barrier = pltpu.get_barrier_semaphore()
+    for partner in partners:
+        pl.semaphore_signal(barrier, inc=1, device_id=partner, device_id_type=MESH)
+    chunks[32 + group] = prepare(geom, density, velocity, pressure, live, pair, line, place)
+    pl.semaphore_wait(barrier, len(partners))
+
+    def copy(start, count, to, device, send, recv):
+        return pltpu.make_async_remote_copy(
+            src_ref=chunks.at[pl.ds(start, count)],
+            dst_ref=chunks.at[pl.ds(to, count)],
+            send_sem=send,
+            recv_sem=recv,
+            device_id=device,
+            device_id_type=MESH,
+        )
+
+    def along_x(k):
+        return copy(32 + group, 1, 32 + group, column(k), x_send.at[k - 1], x_recv.at[k - 1])
+
+    def bundle(step):
+        return 32 + (z + 16 + step) % 8 * 4
+
+    def along_z(step, t):
+        start = bundle(-step * t)
+        if t == 3:
+            start = start + (0 if step > 0 else 2)
+        side = 0 if step > 0 else 1
+        count = 2 if t == 3 else 4
+        return copy(start, count, start, plane(step), z_send.at[side, t], z_recv.at[side, t])
+
+    def arrived_z(step, t):
+        start = bundle(-step * (t + 1))
+        if t == 3:
+            start = start + (0 if step > 0 else 2)
+        side = 0 if step > 0 else 1
+        count = 2 if t == 3 else 4
+        return copy(start, count, start, plane(step), z_send.at[side, t], z_recv.at[side, t])
+
+    def along_r(step, k):
+        side = 0 if step > 0 else 1
+        to = bundle(k) + (-32 if step > 0 else 32)
+        return copy(bundle(k), 4, to, slab(step), r_send.at[side, k], r_recv.at[side, k])
+
+    def arrived_r(step, k):
+        side = 0 if step > 0 else 1
+        to = bundle(k) + (-32 if step > 0 else 32)
+        return copy(to, 4, to, slab(step), r_send.at[side, k], r_recv.at[side, k])
+
+    def give(k):
+        for step in (1, -1):
+            along_r(step, k % 8).start()
+
+    for k in (2, 1, 3):
+        along_x(k).start()
+    for k in (1, 2, 3):
+        begin = 32 + z * 4 + (x + 4 - k) % 4
+        copy(begin, 1, begin, column(k), x_send.at[k - 1], x_recv.at[k - 1]).wait_recv()
+    along_z(1, 0).start()
+    along_z(-1, 0).start()
+    give(0)
+    for t in range(3):
+        for step in (1, -1):
+            arrived_z(step, t).wait_recv()
+            along_z(step, t + 1).start()
+            give(-step * (t + 1))
+    arrived_z(1, 3).wait_recv()
+    arrived_z(-1, 3).wait_recv()
+    give(4)
+    for k in range(8):
+        arrived_r(1, k).wait_recv()
+        arrived_r(-1, k).wait_recv()
+    read_lists(chunks, lists, region, group)
+    for k in (1, 2, 3):
+        along_x(k).wait_send()
+    for t in range(4):
+        along_z(1, t).wait_send()
+        along_z(-1, t).wait_send()
+    for k in range(8):
+        along_r(1, k).wait_send()
+        along_r(-1, k).wait_send()
+
+
+def exchange_call(geom, density, velocity, pressure, live, pair):
     vmem = pl.BlockSpec(memory_space=pltpu.VMEM)
     smem = pl.BlockSpec(memory_space=pltpu.SMEM)
+    dma = pltpu.SemaphoreType.DMA
     return pl.pallas_call(
-        prepare,
-        out_shape=(jax.ShapeDtypeStruct((40, 128), F32), jax.ShapeDtypeStruct((8, 512), F32)),
+        exchange,
+        out_shape=(
+            jax.ShapeDtypeStruct((96, 40, 128), F32),
+            jax.ShapeDtypeStruct((8, 512), F32),
+            jax.ShapeDtypeStruct((32, 128), jnp.int32),
+        ),
         in_specs=[vmem, vmem, vmem, vmem, smem, vmem],
-        out_specs=(vmem, vmem),
-        name="site_order",
-    )(geom, density[None], velocity, pressure[None], live, pair)
-
-
-def make_lines(rows, own, region):
-    lanes = iota(rows.shape, 1)
-    kind = (lanes - CODE) % 3
-    scale = jnp.where(kind == 0, 0.25, 0.125)
-    weight = jnp.where(kind == 0, 1024.0, jnp.where(kind == 1, 32.0, 1.0))
-    origin = jnp.where(lanes[0:1] >= CODE + 3, jnp.roll(own, 3, axis=1), own)
-    steps = jnp.floor((rows - origin) * scale + 0.5) * weight
-    steps = steps + jnp.roll(steps, -1, axis=1) + jnp.roll(steps, -2, axis=1)
-    whole = jnp.where(lanes < CODE, rows, steps).astype(jnp.int32)
-    return whole
+        out_specs=(vmem, vmem, vmem),
+        scratch_shapes=[
+            pltpu.VMEM((8, 128), F32),
+            dma((3,)),
+            dma((3,)),
+            dma((2, 4)),
+            dma((2, 4)),
+            dma((2, 8)),
+            dma((2, 8)),
+        ],
+        compiler_params=pltpu.CompilerParams(
+            collective_id=0, has_side_effects=True, vmem_limit_bytes=16 * 1024 * 1024
+        ),
+        name="gather_sites",
+    )(geom, density[None], velocity, pressure[None], live, pair.T)
 
 
 def locate(block, region):
     owner = block // 2
-    layer = owner // 32 - region + 1
-    return layer, (owner % 32) * LAYERS + layer, block % 2
+    return owner // 32 - region + 1, owner % 32, block % 2
 
 
 def direction(step):
@@ -107,7 +226,7 @@
     return valid, a * 9 + b * 3 + c
 
 
-def fill_tables(lines, region, own, source, used, faces, face_used):
+def fill_tables(lists, region, group, source, used, faces, face_used):
     def clear(k, _):
         source[k] = -1
         return _
@@ -123,16 +242,18 @@
 
     lax.fori_loop(0, 27, clear_dir, 0, unroll=9)
 
+    def code(g, layer, s):
+        return lists[g, layer * 32 + 28 + 3 * s]
+
     def slot(p, _):
-        head = lines[own, HEAD + p]
-        tail = lines[own, TAIL + p]
+        head = lists[group, 32 + p]
+        tail = lists[group, 32 + LIST + p]
 
         @pl.when(head >= 0)
         def _row():
-            _, at, s = locate(tail, region)
-            place = lines[at, CODE + 3 * s]
-            home = lines[own, CODE + 3 * (head % 2)]
-            valid, way = direction(place - home)
+            layer, g, s = locate(tail, region)
+            place = code(g, layer, s)
+            valid, way = direction(place - code(group, 1, head % 2))
 
             @pl.when(valid)
             def _face():
@@ -140,16 +261,16 @@
                 face_used[way] = 1
 
             def entry(k, _):
-                @pl.when(lines[at, HEAD + k] == tail)
+                @pl.when(lists[g, layer * 32 + k] == tail)
                 def _listed():
-                    layer, there, t = locate(lines[at, TAIL + k], region)
-                    near = (layer >= 0) & (layer < LAYERS)
-                    there = jnp.where(near, there, 0)
-                    fits, towards = direction(lines[there, CODE + 3 * t] - place)
+                    wide, there, t = locate(lists[g, layer * 32 + LIST + k], region)
+                    near = (wide >= 0) & (wide < LAYERS)
+                    wide = jnp.where(near, wide, 1)
+                    fits, towards = direction(code(there, wide, t) - place)
 
                     @pl.when(fits & near)
                     def _set():
-                        source[towards * 16 + p] = there * 2 + t
+                        source[towards * 16 + p] = (wide * 32 + there) * 2 + t
                         used[towards] = 1
 
                 return _
@@ -161,7 +282,7 @@
     lax.fori_loop(0, LIST, slot, 0)
 
 
-def gather_sites(chunks, source, used, near):
+def collect_sites(chunks, source, used, near):
     group = iota((8, 128), 1) // 8
 
     def one_way(way, _):
@@ -437,12 +558,12 @@
 
 
 def sweep(
-    lines, chunks, place, gradients, rate, source, used, faces, face_used, near, halo, fields,
+    lists, chunks, place, gradients, rate, source, used, faces, face_used, near, halo, fields,
     around, wide,
 ):
-    region, own = lines[0, 126], lines[0, 127]
-    fill_tables(lines, region, own, source, used, faces, face_used)
-    gather_sites(chunks, source, used, near)
+    region, group = lists[0, 96], lists[0, 97]
+    fill_tables(lists, region, group, source, used, faces, face_used)
+    collect_sites(chunks, source, used, near)
     shift_sites(near, halo)
     moments(near, halo, fields)
     gather_fields(fields, faces, face_used, around)
@@ -464,7 +585,7 @@
             rate[k - 15 : k - 14, :] = row
 
 
-def sweep_call(lines, chunks, place):
+def sweep_call(lists, chunks, place):
     vmem = pl.BlockSpec(memory_space=pltpu.VMEM)
     smem = pl.BlockSpec(memory_space=pltpu.SMEM)
     return pl.pallas_call(
@@ -485,26 +606,12 @@
         ],
         compiler_params=pltpu.CompilerParams(vmem_limit_bytes=48 * 1024 * 1024),
         name="sweep",
-    )(lines, chunks, place)
-
-
-def beside(chunk):
-    count = lax.axis_size("region")
-    up = [(i, i + 1) for i in range(count - 1)]
-    down = [(i + 1, i) for i in range(count - 1)]
-    below, above = lax.ppermute(chunk, "region", up), lax.ppermute(chunk, "region", down)
-    return jnp.stack([below, chunk, above])
+    )(lists, chunks, place)
 
 
 def body(geom, density, velocity, pressure, block_live, pair_list):
-    chunk, place = prepare_call(geom, density, velocity, pressure, block_live, pair_list)
-    chunks = lax.all_gather(beside(chunk), "group", axis=0, tiled=True)
-    region = lax.axis_index("region")
-    own = lax.axis_index("group") * LAYERS + 1
-    lines = make_lines(chunks[:, 32, :], chunk[32:33, :], region)
-    tag = jnp.where(iota((1, 128), 1) == 126, region, own)
-    lines = jnp.where(iota(lines.shape, 1) >= 126, tag, lines)
-    return sweep_call(lines, chunks, place)
+    chunks, place, lists = exchange_call(geom, density, velocity, pressure, block_live, pair_list)
+    return sweep_call(lists, chunks, place)
 
 
 def solution(mesh):

time: 163 us -> 80.9 us (0.50)
  the two profiles are of different devices: /device:TPU:24 before, /device:TPU:49 now
where the time goes in v2:
time: 80.9 us; the launch traced here: 80.6 us
  Pallas kernels  75.9 us (94%)
  local copies, waits for them, and re-layouts  4.08 us (5%)
    pallas_call x1, Pallas kernels, sweep_call(): pl.pallas_call(sweep, out_shape=(jax.ShapeDtypeStruct((15, 512), F32), ja...  42.4 us
    pallas_call x1, Pallas kernels, exchange_call(): pl.pallas_call(exchange, out_shape=(jax.ShapeDtypeStruct((96, 40, 128), F...  33.4 us
    unnamed x12, local copies, waits for them, and re-layouts  4.08 us

profile of v2, /device:TPU:49, one launch (start us, length us, event | category | flops | bytes accessed | tf_op | source)
XLA Modules:
  0.0 80.6 jit_solution(16376140170951644669)
XLA Ops:
  0.6 0.0 copy-start
  0.6 0.7 copy-done
  1.3 0.0 copy-start.1
  1.3 0.7 copy-done.1
  2.0 0.0 copy-start.2
  2.0 0.7 copy-done.2
  2.7 0.0 copy-start.3
  2.7 0.7 copy-done.3
  3.4 0.0 copy-start.4
  3.4 0.7 copy-done.4
  4.1 0.0 copy-start.5
  4.1 0.7 copy-done.5
  4.7 33.4 %gather_sites.1 = (f32[96,40,128]{2,1,0:T(8,128)S(1)}, f32[8,512]{1,0:T(8,128)S(1)}, s32[32,128]{1,0:T(8,128)S(1)}) custom-call(f32[4,512]{1,0:T(4,128)S(1)} %copy-done, f32[1,512]{1,0:T(1,128)S(1)} %bitcast.3, f32[3,512]{1,0:T(4,128)S(1)} %copy-done.1, f32[1,512]{1,0:T(1,128)S(1)} %bitcast.4, s32[2]{0:T(128)S(1)} %copy-done.5, s32[2,14]{1,0:T(2,128)S(1)} %bitcast.5), custom_call_target="tpu_custom_call" | custom-call | tf_op jit(solution)/shard_map/gather_sites/pallas_call | solution.py:192
  38.1 42.4 %sweep.1 = (f32[15,512]{1,0:T(8,128)}, f32[5,512]{1,0:T(8,128)}) custom-call(s32[32,128]{1,0:T(8,128)S(1)} %get-tuple-element.5.lists, f32[96,40,128]{2,1,0:T(8,128)S(1)} %get-tuple-element.6.chunks, f32[8,512]{1,0:T(8,128)S(1)} %get-tuple-element.7.place), custom_call_target="tpu_custom_call" | custom-call | tf_op jit(solution)/shard_map/sweep/pallas_call | solution.py:591
Async XLA Ops:
  0.6 0.7 copy-start
  1.3 0.7 copy-start.1
  2.0 0.7 copy-start.2
  2.7 0.7 copy-start.3
  3.4 0.7 copy-start.4
  4.1 0.7 copy-start.5

commit v3 on v2

--- a/solution.py
+++ b/solution.py
@@ -70,19 +70,22 @@
 
 
 def read_lists(chunks, lists, region, group):
-    lanes = iota((32, 128), 1)
+    lanes = iota((24, 128), 1)
     kind = (lanes - CORNER) % 3
     scale = jnp.where(kind == 0, 0.25, 0.125)
     weight = jnp.where(kind == 0, 1024.0, jnp.where(kind == 1, 32.0, 1.0))
     own = chunks[32 + group, 32:33, :]
     own = jnp.where(lanes[0:1] >= CORNER + 3, pltpu.roll(own, 3, 1), own)
-    whole = jnp.where(lanes == 96, region, group)
-    for layer in range(LAYERS):
-        rows = chunks[32 * layer : 32 * layer + 32, 32, :]
+    first = ((region - 1) * 64).astype(F32)
+    whole = jnp.zeros((24, 128), jnp.int32)
+    for m in range(4):
+        rows = chunks[pl.ds(m, 24, stride=4), 32, :]
         steps = jnp.floor((rows - own) * scale + 0.5) * weight
         steps = steps + pltpu.roll(steps, 127, 1) + pltpu.roll(steps, 126, 1)
-        rows = pltpu.roll(jnp.where(lanes < CORNER, rows, steps), 64 + 32 * layer, 1)
-        whole = jnp.where(lanes // 32 == layer, rows.astype(jnp.int32), whole)
+        ids = jnp.where(rows < 0.0, -1.0, rows - first)
+        rows = jnp.where(lanes < CORNER, ids, steps).astype(jnp.int32)
+        rows = jnp.where(lanes == CORNER + 1, region, jnp.where(lanes == CORNER + 2, group, rows))
+        whole = jnp.where(lanes // 32 == m, pltpu.roll(rows, (64 + 32 * m) % 128, 1), whole)
     lists[...] = whole
 
 
@@ -194,7 +197,7 @@
         out_shape=(
             jax.ShapeDtypeStruct((96, 40, 128), F32),
             jax.ShapeDtypeStruct((8, 512), F32),
-            jax.ShapeDtypeStruct((32, 128), jnp.int32),
+            jax.ShapeDtypeStruct((24, 128), jnp.int32),
         ),
         in_specs=[vmem, vmem, vmem, vmem, smem, vmem],
         out_specs=(vmem, vmem, vmem),
@@ -214,102 +217,95 @@
     )(geom, density[None], velocity, pressure[None], live, pair.T)
 
 
-def locate(block, region):
-    owner = block // 2
-    return owner // 32 - region + 1, owner % 32, block % 2
-
-
-def direction(step):
+def direction(step, wanted):
     u = step + 1057
     a, b, c = u >> 10, (u >> 5) & 31, u & 31
-    valid = (u >= 0) & (a <= 2) & (b <= 2) & (c <= 2)
-    return valid, a * 9 + b * 3 + c
-
-
-def fill_tables(lists, region, group, source, used, faces, face_used):
+    fits = wanted & (u >= 0) & (jnp.maximum(jnp.maximum(a, b), c) <= 2)
+    return jnp.where(fits, a * 9 + b * 3 + c, 27)
+
+
+def fill_tables(lists, source, used, faces, face_used):
     def clear(k, _):
         source[k] = -1
         return _
 
     lax.fori_loop(0, 27 * 16, clear, 0, unroll=16)
 
-    def clear_dir(k, _):
+    def clear_way(k, _):
         used[k] = 0
         face_used[k] = 0
         faces[k] = -1
-        faces[27 + k] = -1
-        return _
-
-    lax.fori_loop(0, 27, clear_dir, 0, unroll=9)
-
-    def code(g, layer, s):
-        return lists[g, layer * 32 + 28 + 3 * s]
+        faces[28 + k] = -1
+        return _
+
+    lax.fori_loop(0, 28, clear_way, 0, unroll=14)
+    own = (32 + lists[30]) * 32
+
+    def code(block):
+        return lists[(block >> 1) * 32 + 28 + 3 * (block & 1)]
 
     def slot(p, _):
-        head = lists[group, 32 + p]
-        tail = lists[group, 32 + LIST + p]
-
-        @pl.when(head >= 0)
-        def _row():
-            layer, g, s = locate(tail, region)
-            place = code(g, layer, s)
-            valid, way = direction(place - code(group, 1, head % 2))
-
-            @pl.when(valid)
-            def _face():
-                faces[(head % 2) * 27 + way] = p
-                face_used[way] = 1
-
-            def entry(k, _):
-                @pl.when(lists[g, layer * 32 + k] == tail)
-                def _listed():
-                    wide, there, t = locate(lists[g, layer * 32 + LIST + k], region)
-                    near = (wide >= 0) & (wide < LAYERS)
-                    wide = jnp.where(near, wide, 1)
-                    fits, towards = direction(code(there, wide, t) - place)
-
-                    @pl.when(fits & near)
-                    def _set():
-                        source[towards * 16 + p] = (wide * 32 + there) * 2 + t
-                        used[towards] = 1
-
-                return _
-
-            lax.fori_loop(0, LIST, entry, 0)
-
+        head = lists[own + p]
+        listed = head >= 0
+        tail = jnp.where(listed, lists[own + LIST + p], 64)
+        place = code(tail)
+        way = direction(place - lists[own + 28 + 3 * (head & 1)], listed)
+        faces[(head & 1) * 28 + way] = p
+        face_used[way] = 1
+        at = (tail >> 1) * 32
+        for k in range(LIST):
+            there = lists[at + LIST + k]
+            near = listed & (lists[at + k] == tail) & (there >= 0) & (there < 192)
+            there = jnp.where(near, there, 0)
+            towards = direction(code(there) - place, near)
+            source[towards * 16 + p] = there
+            used[towards] = 1
         return _
 
     lax.fori_loop(0, LIST, slot, 0)
+
+
+def swap(low, high, is_low, width):
+    first = jnp.where(is_low, low, pltpu.roll(high, width, 1))
+    second = jnp.where(is_low, pltpu.roll(low, 128 - width, 1), high)
+    return first, second
 
 
 def collect_sites(chunks, source, used, near):
     group = iota((8, 128), 1) // 8
+    bit = [(group >> k) % 2 == 0 for k in range(4)]
 
     def one_way(way, _):
         @pl.when(used[way] > 0)
         def _present():
             froms = [source[way * 16 + p] for p in range(LIST)]
-            wanted = [jnp.where(f >= 0, p, -1) for p, f in enumerate(froms)]
-            froms = [jnp.maximum(f, 0) for f in froms]
-
-            def one_tile(t, _):
-                sums = [jnp.zeros((8, 128), F32) for _k in range(8)]
-                for p in range(LIST):
-                    tile = chunks[froms[p] // 2, pl.ds(pl.multiple_of(t * 8, 8), 8), :]
-                    tile = pltpu.roll(tile, (froms[p] % 2) * 96 + p * 8, 1)
-                    mask = group == wanted[p]
-                    for k in range(8):
-                        moved = pltpu.roll(tile, (128 - 64 * (k // 4) - 8 * (k % 4)) % 128, 1)
-                        sums[k] = jnp.where(mask, moved, sums[k])
-                for k in range(8):
-                    near[way, 2 * t + k // 4, k % 4] = sums[k]
-                return _
-
-            lax.fori_loop(0, 5, one_tile, 0)
-            for x in range(4):
-                radius = near[way, 8, x]
-                near[way, 9, x] = radius
-                near[way, 8, x] = jnp.where(radius > 0.0, 1.0, 0.0)
+            there = jnp.zeros((8, 128), jnp.int32)
+            second = jnp.zeros((8, 128), jnp.int32)
+            for p in range(LIST):
+                mask = group == p
+                there = jnp.where(mask, jnp.where(froms[p] >= 0, 1, 0), there)
+                second = jnp.where(mask, froms[p] & 1, second)
+            there, second = there > 0, second > 0
+            at = [jnp.maximum(f, 0) >> 1 for f in froms]
+            at += [at[0], at[1]]
+            for t in range(5):
+                v = [chunks[at[p], 8 * t : 8 * t + 8, :] for p in range(16)]
+                for k in (0, 1, 3):
+                    step = 1 << k
+                    for p in range(16):
+                        if not p & step:
+                            v[p], v[p + step] = swap(v[p], v[p + step], bit[k], 8 * step)
+                for n in range(8):
+                    par, x = n // 4, n % 4
+                    low, high = v[8 * par + x], v[8 * par + x + 4]
+                    low = jnp.where(second, pltpu.roll(low, 96, 1), low)
+                    high = jnp.where(second, high, pltpu.roll(high, 32, 1))
+                    out = jnp.where(there, jnp.where(bit[2], low, high), 0.0)
+                    if 2 * t + par == 8:
+                        near[way, 9, x] = out
+                        out = jnp.where(out > 0.0, 1.0, 0.0)
+                    if 2 * t + par < 9:
+                        near[way, 2 * t + par, x] = out
 
         @pl.when(used[way] == 0)
         def _absent():
@@ -331,16 +327,21 @@
 
 def shift_sites(near, halo):
     z = iota((8, 128), 1) % 8
+    upper = iota((8, 128), 0) < 4
 
     def one_row(row, _):
         for xe in range(8):
             sx, x = (0, xe + 2) if xe < 2 else (1, xe - 2) if xe < 6 else (2, xe - 6)
-            for sy in range(3):
-                base, below, above = [near[sx * 9 + sy * 3 + sz, row, x] for sz in (1, 0, 2)]
-                for dz in range(-2, 3):
-                    halo[dz + 2, row, xe, 8 * sy : 8 * sy + 8, :] = shifted(
-                        base, below, above, z, dz
-                    )
+            mid = [near[sx * 9 + 3 + sz, row, x] for sz in (1, 0, 2)]
+            rim = [
+                jnp.where(upper, near[sx * 9 + 6 + sz, row, x], near[sx * 9 + sz, row, x])
+                for sz in (1, 0, 2)
+            ]
+            for dz in range(-2, 3):
+                halo[dz + 2, row, xe, 8:16, :] = shifted(*mid, z, dz)
+                edge = shifted(*rim, z, dz)
+                halo[dz + 2, row, xe, 0:8, :] = edge
+                halo[dz + 2, row, xe, 16:24, :] = edge
         return _
 
     lax.fori_loop(0, 9, one_row, 0)
@@ -399,10 +400,11 @@
             rows.append(b[0] * f[0] + b[3] * f[1] + b[4] * f[2])
             rows.append(b[3] * f[0] + b[1] * f[1] + b[5] * f[2])
             rows.append(b[4] * f[0] + b[5] * f[1] + b[2] * f[2])
-        for k in range(10):
-            pair = jnp.concatenate(rows[3 * k : 3 * k + 3], axis=0)
+        at = pl.ds(pl.multiple_of(x * 128, 128), 128)
+        for k in range(15):
+            pair = jnp.concatenate(rows[2 * k : 2 * k + 2], axis=0)
             for n, part in enumerate(split3(pair)):
-                fields[x, n, 24 * k : 24 * k + 24, :] = part.astype(F32)
+                fields[240 * n + 16 * k : 240 * n + 16 * k + 16, at] = part
         return _
 
     lax.fori_loop(0, 4, one_plane, 0)
@@ -420,20 +422,19 @@
 
         @pl.when(any_used > 0)
         def _present():
-            total = jnp.zeros((240, 128), F32)
+            hot = []
             for x in range(4):
                 wanted = jnp.full((1, 128), -1, jnp.int32)
                 for sx, xe in ((1, x + 2), (2, x + 6) if x < 2 else (0, x - 2)):
                     for s in range(2):
-                        p = faces[s * 27 + sx * 9 + sy * 3 + sz]
+                        p = faces[s * 28 + sx * 9 + sy * 3 + sz]
                         lane = jnp.where(p >= 0, p * 8 + z, -1)
                         wanted = jnp.where(lanes // 8 == xe * 2 + s, lane, wanted)
-                hot = jnp.where(sources == wanted, 1.0, 0.0).astype(BF16)
-                for k in range(3):
-                    total = total + jnp.dot(
-                        fields[x, k].astype(BF16), hot, preferred_element_type=F32
-                    )
-            around[n] = total
+                hot.append(jnp.where(sources == wanted, 1.0, 0.0).astype(BF16))
+            found = jnp.dot(
+                fields[...], jnp.concatenate(hot, axis=0), preferred_element_type=F32
+            )
+            around[n] = found[0:240] + found[240:480] + found[480:720]
 
         @pl.when(any_used == 0)
         def _absent():
@@ -444,25 +445,43 @@
     lax.fori_loop(0, 9, one_way, 0)
 
 
-def shift_fields(around, wide):
+def shift_fields(around, wide, inner):
     lanes = iota((8, 128), 1)
     z = lanes % 8
+    outer = (lanes < 16) | (lanes >= 112)
+    middle = (lanes >= 32) & (lanes < 96)
     left = lanes < 64
-
-    def one_row(row, _):
-        at = pl.ds(pl.multiple_of(row * 8, 8), 8)
-        for sy in range(3):
-            base, below, above = [around[sz * 3 + sy, at, :] for sz in (1, 0, 2)]
-            for dz in range(-2, 3):
-                far = shifted(base, below, above, z, dz)
-                rows = slice(8 * sy, 8 * sy + 8)
-                wide[dz + 2, 0, row, rows, :] = far
-                for k, step in ((1, 16), (2, 32)):
-                    both = jnp.where(left, pltpu.roll(far, 128 - step, 1), pltpu.roll(far, step, 1))
-                    wide[dz + 2, k, row, rows, :] = both
-        return _
-
-    lax.fori_loop(0, 30, one_row, 0)
+    upper = iota((8, 128), 0) < 4
+
+    def some_rows(n, _):
+        for m in range(3):
+            row = n * 3 + m
+            at = pl.ds(pl.multiple_of(row * 8, 8), 8)
+            mid = [around[sz * 3 + 1, at, :] for sz in (1, 0, 2)]
+            rim = [
+                jnp.where(upper, around[sz * 3 + 2, at, :], around[sz * 3, at, :])
+                for sz in (1, 0, 2)
+            ]
+            for is_rim, parts in ((False, mid), (True, rim)):
+                for dz in range(-2, 3):
+                    far = shifted(*parts, z, dz)
+                    half = pltpu.roll(far, 64, 1)
+                    orders = far, jnp.where(outer, half, far), jnp.where(middle, far, half)
+                    for k, value in enumerate(orders):
+                        if is_rim:
+                            wide[dz + 2, k, row, 0:8, :] = value
+                            wide[dz + 2, k, row, 16:24, :] = value
+                        else:
+                            wide[dz + 2, k, row, 8:16, :] = value
+                    if dz == 0 and not is_rim:
+                        own = orders[2]
+                        back, on = pltpu.roll(own, 112, 1), pltpu.roll(own, 16, 1)
+                        inner[0, row] = pltpu.roll(own, 32, 1)
+                        inner[1, row] = jnp.where(left, back, on)
+                        inner[2, row] = own
+        return _
+
+    lax.fori_loop(0, 10, some_rows, 0)
 
 
 def weight(scaled):
@@ -527,51 +546,58 @@
     return [jnp.where(live, t * area, 0.0) for t in terms + [heat]]
 
 
-def fluxes(wide):
-    half = iota((8, 128), 1) < 64
-
-    def near(row):
-        return wide[2, 2, row, 8:16, :]
-
-    def add(sums, far):
-        return tuple(a + b for a, b in zip(sums, face(near, far)))
+def fluxes(wide, inner):
+    left = iota((8, 128), 1) < 64
+
+    def add(order, sums, far):
+        return tuple(a + b for a, b in zip(sums, face(lambda row: inner[order, row], far)))
 
     def step(dz, sums):
+        sums = list(sums)
         for k in range(2):
             for dy in range(-2, 3):
-                sums = add(sums, lambda row: wide[dz, k, row, 8 + dy : 16 + dy, :])
+                sums[k] = add(k, sums[k], lambda row: wide[dz, k, row, 8 + dy : 16 + dy, :])
         for d in (-2, 1):
-            sums = add(
-                sums,
+            sums[2] = add(
+                2,
+                sums[2],
                 lambda row: jnp.where(
-                    half, wide[dz, 2, row, 8 + d : 16 + d, :], wide[dz, 2, row, 9 + d : 17 + d, :]
+                    left, wide[dz, 2, row, 8 + d : 16 + d, :], wide[dz, 2, row, 9 + d : 17 + d, :]
                 ),
             )
-        return sums
-
-    sums = lax.fori_loop(0, 5, step, (jnp.zeros((8, 128), F32),) * 5)
+        return tuple(sums)
+
+    zero = (jnp.zeros((8, 128), F32),) * 5
+    two, one, same = lax.fori_loop(0, 5, step, (zero, zero, zero))
     for d in (0, 1):
-        sums = add(
-            sums, lambda row: jnp.where(half, wide[d, 2, row, 8:16, :], wide[4 - d, 2, row, 8:16, :])
+        same = add(
+            2,
+            same,
+            lambda row: jnp.where(left, wide[d, 2, row, 8:16, :], wide[4 - d, 2, row, 8:16, :]),
         )
-    return [-(v + pltpu.roll(v, 64, 1)) for v in sums]
+    found = []
+    for a, b, c in zip(two, one, same):
+        total = c + pltpu.roll(a, 32, 1)
+        total = total + pltpu.roll(jnp.where(left, b, 0.0), 16, 1)
+        total = total + pltpu.roll(jnp.where(left, 0.0, b), 112, 1)
+        found.append(-(total + pltpu.roll(total, 64, 1)))
+    return found
 
 
 def sweep(
     lists, chunks, place, gradients, rate, source, used, faces, face_used, near, halo, fields,
-    around, wide,
+    around, wide, inner,
 ):
-    region, group = lists[0, 96], lists[0, 97]
-    fill_tables(lists, region, group, source, used, faces, face_used)
+    fill_tables(lists, source, used, faces, face_used)
     collect_sites(chunks, source, used, near)
     shift_sites(near, halo)
     moments(near, halo, fields)
     gather_fields(fields, faces, face_used, around)
-    shift_fields(around, wide)
-    rates = fluxes(wide)
-    rows = [wide[2, 2, 15 + k, 8:16, :] for k in range(15)] + rates
+    shift_fields(around, wide, inner)
+    rates = fluxes(wide, inner)
+    rows = [wide[2, 0, 15 + k, 8:16, :] for k in range(15)] + rates
     found = jnp.concatenate(rows, axis=0)
-    lane = place[1:2, :].astype(jnp.int32)
+    lane = place[1:2, :].astype(jnp.int32) + 32
     hot = jnp.where(iota((128, 512), 0) == lane, 1.0, 0.0).astype(BF16)
     total = jnp.zeros((160, 512), F32)
     for part in split3(found):
@@ -594,19 +620,20 @@
         in_specs=[smem, vmem, vmem],
         out_specs=(vmem, vmem),
         scratch_shapes=[
-            pltpu.SMEM((27 * 16,), jnp.int32),
-            pltpu.SMEM((27,), jnp.int32),
-            pltpu.SMEM((54,), jnp.int32),
-            pltpu.SMEM((27,), jnp.int32),
+            pltpu.SMEM((28 * 16,), jnp.int32),
+            pltpu.SMEM((28,), jnp.int32),
+            pltpu.SMEM((56,), jnp.int32),
+            pltpu.SMEM((28,), jnp.int32),
             pltpu.VMEM((27, 10, 4, 8, 128), F32),
             pltpu.VMEM((5, 9, 8, 24, 128), F32),
-            pltpu.VMEM((4, 3, 240, 128), F32),
+            pltpu.VMEM((720, 512), BF16),
             pltpu.VMEM((9, 240, 128), F32),
             pltpu.VMEM((5, 3, 30, 24, 128), F32),
+            pltpu.VMEM((3, 30, 8, 128), F32),
         ],
         compiler_params=pltpu.CompilerParams(vmem_limit_bytes=48 * 1024 * 1024),
         name="sweep",
-    )(lists, chunks, place)
+    )(lists.reshape(24 * 128), chunks, place)
 
 
 def body(geom, density, velocity, pressure, block_live, pair_list):

time: 80.9 us -> 66.2 us (0.82)
  the two profiles are of different devices: /device:TPU:49 before, /device:TPU:25 now
where the time goes in v3:
time: 66.2 us; the launch traced here: 65.9 us
  Pallas kernels  61.2 us (92%)
  local copies, waits for them, and re-layouts  4.08 us (6%)
    pallas_call x1, Pallas kernels, exchange_call(): pl.pallas_call(exchange, out_shape=(jax.ShapeDtypeStruct((96, 40, 128), F...  35.5 us
    pallas_call x1, Pallas kernels, sweep_call(): pl.pallas_call(sweep, out_shape=(jax.ShapeDtypeStruct((15, 512), F32), ja...  25.7 us
    unnamed x12, local copies, waits for them, and re-layouts  4.08 us

profile of v3, /device:TPU:25, one launch (start us, length us, event | category | flops | bytes accessed | tf_op | source)
XLA Modules:
  0.0 65.9 jit_solution(9463696569891067810)
XLA Ops:
  0.6 0.0 copy-start
  0.6 0.7 %copy-done = f32[4,512]{1,0:T(4,128)S(1)} copy-done((f32[4,512]{1,0:T(4,128)S(1)}, f32[4,512]{1,0:T(4,128)}, u32[]{:S(2)}) %copy-start) | copy-done | bytes 8216
  1.3 0.0 copy-start.1
  1.3 0.7 %copy-done.1 = f32[3,512]{1,0:T(4,128)S(1)} copy-done((f32[3,512]{1,0:T(4,128)S(1)}, f32[3,512]{1,0:T(4,128)}, u32[]{:S(2)}) %copy-start.1) | copy-done | bytes 6168
  2.0 0.0 copy-start.2
  2.0 0.7 %copy-done.2 = f32[512]{0:T(512)S(1)} copy-done((f32[512]{0:T(512)S(1)}, f32[512]{0:T(512)}, u32[]{:S(2)}) %copy-start.2) | copy-done | bytes 2072
  2.7 0.0 copy-start.3
  2.7 0.7 %copy-done.3 = f32[512]{0:T(512)S(1)} copy-done((f32[512]{0:T(512)S(1)}, f32[512]{0:T(512)}, u32[]{:S(2)}) %copy-start.3) | copy-done | bytes 2072
  3.4 0.0 copy-start.4
  3.4 0.7 %copy-done.4 = s32[14,2]{0,1:T(2,128)S(1)} copy-done((s32[14,2]{0,1:T(2,128)S(1)}, s32[14,2]{0,1:T(2,128)}, u32[]{:S(2)}) %copy-start.4) | copy-done | bytes 136
  4.1 0.0 copy-start.5
  4.1 0.7 copy-done.5
  4.7 35.5 %gather_sites.1 = (f32[96,40,128]{2,1,0:T(8,128)S(1)}, f32[8,512]{1,0:T(8,128)S(1)}, s32[24,128]{1,0:T(8,128)S(1)}) custom-call(f32[4,512]{1,0:T(4,128)S(1)} %copy-done, f32[1,512]{1,0:T(1,128)S(1)} %bitcast.5, f32[3,512]{1,0:T(4,128)S(1)} %copy-done.1, f32[1,512]{1,0:T(1,128)S(1)} %bitcast.6, s32[2]{0:T(128)S(1)} %copy-done.5, s32[2,14]{1,0:T(2,128)S(1)} %bitcast.7), custom_call_target="tpu_custom_call" | custom-call | tf_op jit(solution)/shard_map/gather_sites/pallas_call | solution.py:195
  40.3 25.7 %sweep.1 = (f32[15,512]{1,0:T(8,128)}, f32[5,512]{1,0:T(8,128)}) custom-call(s32[3072]{0:T(1024)S(1)} %bitcast.4, f32[96,40,128]{2,1,0:T(8,128)S(1)} %get-tuple-element.6.chunks, f32[8,512]{1,0:T(8,128)S(1)} %get-tuple-element.7.place), custom_call_target="tpu_custom_call" | custom-call | tf_op jit(solution)/shard_map/sweep/pallas_call | solution.py:617
Async XLA Ops:
  0.6 0.7 %copy-start = (f32[4,512]{1,0:T(4,128)S(1)}, f32[4,512]{1,0:T(4,128)}, u32[]{:S(2)}) copy-start(f32[4,512]{1,0:T(4,128)} %geom.1) | copy-start | bytes 24580
  1.3 0.7 %copy-start.1 = (f32[3,512]{1,0:T(4,128)S(1)}, f32[3,512]{1,0:T(4,128)}, u32[]{:S(2)}) copy-start(f32[3,512]{1,0:T(4,128)} %velocity.1) | copy-start | bytes 18436
  2.0 0.7 %copy-start.2 = (f32[512]{0:T(512)S(1)}, f32[512]{0:T(512)}, u32[]{:S(2)}) copy-start(f32[512]{0:T(512)} %param.7) | copy-start | bytes 6148
  2.7 0.7 %copy-start.3 = (f32[512]{0:T(512)S(1)}, f32[512]{0:T(512)}, u32[]{:S(2)}) copy-start(f32[512]{0:T(512)} %param.9) | copy-start | bytes 6148
  3.4 0.7 %copy-start.4 = (s32[14,2]{0,1:T(2,128)S(1)}, s32[14,2]{0,1:T(2,128)}, u32[]{:S(2)}) copy-start(s32[14,2]{0,1:T(2,128)} %param.11) | copy-start | bytes 340
  4.1 0.7 copy-start.5

commit v4 on v3

--- a/solution.py
+++ b/solution.py
@@ -31,16 +31,16 @@
     return high, middle, low
 
 
-def prepare(geom, density, velocity, pressure, live, pair, line, place):
+def prepare(values, line, place):
     lanes = iota((1, 128), 1)
     total = jnp.zeros((40, 128), F32)
     line[...] = jnp.zeros((8, 128), F32)
-    line[0:1, HEAD : HEAD + LIST] = pair[0:1, :].astype(F32)
-    line[0:1, TAIL : TAIL + LIST] = pair[1:2, :].astype(F32)
+    line[0:1, HEAD : HEAD + LIST] = values[9:10, 0:LIST]
+    line[0:1, TAIL : TAIL + LIST] = values[10:11, 0:LIST]
     listed = line[0:1, :]
     for s in range(2):
         at = slice(s * BLOCK, (s + 1) * BLOCK)
-        corner = geom[:, at]
+        corner = values[0:4, at]
         columns = jnp.concatenate([corner, corner], axis=0).T
         cells = []
         for k, count in ((0, 64), (1, 32), (2, 32)):
@@ -50,10 +50,10 @@
             low = jnp.min(corner[k : k + 1, :], axis=1, keepdims=True)
             listed = listed + jnp.where(lanes == CORNER + 3 * s + k, low, 0.0)
         lane = cells[0] * 8 + cells[2]
-        alive = iota((1, BLOCK), 1) < live[s]
-        rows = [corner[0:1], corner[1:2], corner[2:3], jnp.log(density[:, at])]
-        rows += [velocity[k : k + 1, at] for k in range(3)]
-        rows += [jnp.log(pressure[:, at]), jnp.where(alive, corner[3:4], 0.0)]
+        alive = iota((1, BLOCK), 1).astype(F32) < values[11:12, s : s + 1]
+        rows = [corner[0:1], corner[1:2], corner[2:3], jnp.log(values[4:5, at])]
+        rows += [values[5 + k : 6 + k, at] for k in range(3)]
+        rows += [jnp.log(values[8:9, at]), jnp.where(alive, corner[3:4], 0.0)]
         here = iota((8, BLOCK), 0) == cells[1]
         spread = [jnp.where(here, row, 0.0) for row in rows] + [jnp.zeros((8, BLOCK), F32)]
         for par in range(2):
@@ -74,12 +74,12 @@
     kind = (lanes - CORNER) % 3
     scale = jnp.where(kind == 0, 0.25, 0.125)
     weight = jnp.where(kind == 0, 1024.0, jnp.where(kind == 1, 32.0, 1.0))
-    own = chunks[32 + group, 32:33, :]
+    own = chunks[1, group // 4, group % 4, 32:33, :]
     own = jnp.where(lanes[0:1] >= CORNER + 3, pltpu.roll(own, 3, 1), own)
     first = ((region - 1) * 64).astype(F32)
     whole = jnp.zeros((24, 128), jnp.int32)
     for m in range(4):
-        rows = chunks[pl.ds(m, 24, stride=4), 32, :]
+        rows = chunks[:, :, m, 32, :].reshape(24, 128)
         steps = jnp.floor((rows - own) * scale + 0.5) * weight
         steps = steps + pltpu.roll(steps, 127, 1) + pltpu.roll(steps, 126, 1)
         ids = jnp.where(rows < 0.0, -1.0, rows - first)
@@ -89,9 +89,12 @@
     lists[...] = whole
 
 
+STEPS = (1, -1, 2, -2, 3, -3, 4)
+
+
 def exchange(
-    geom, density, velocity, pressure, live, pair, chunks, place, lists, line,
-    x_send, x_recv, z_send, z_recv, r_send, r_recv,
+    values, chunks, place, lists, line,
+    z_send, z_recv, x_send, x_recv, r_send, r_recv,
 ):
     region, group = lax.axis_index("region"), lax.axis_index("group")
     z, x = group // 4, group % 4
@@ -105,108 +108,100 @@
     def slab(step):
         return ((region + 16 + step) % 16, group)
 
-    partners = [column(k) for k in (1, 2, 3)] + [plane(1), plane(-1), slab(1), slab(-1)]
+    partners = [column(k) for k in (1, 2, 3)] + [plane(k) for k in STEPS] + [slab(1), slab(-1)]
     barrier = pltpu.get_barrier_semaphore()
     for partner in partners:
         pl.semaphore_signal(barrier, inc=1, device_id=partner, device_id_type=MESH)
-    chunks[32 + group] = prepare(geom, density, velocity, pressure, live, pair, line, place)
+    chunks[1, z, x] = prepare(values, line, place)
     pl.semaphore_wait(barrier, len(partners))
 
-    def copy(start, count, to, device, send, recv):
+    def copy(source, target, device, send, recv):
         return pltpu.make_async_remote_copy(
-            src_ref=chunks.at[pl.ds(start, count)],
-            dst_ref=chunks.at[pl.ds(to, count)],
+            src_ref=source,
+            dst_ref=target,
             send_sem=send,
             recv_sem=recv,
             device_id=device,
             device_id_type=MESH,
         )
 
-    def along_x(k):
-        return copy(32 + group, 1, 32 + group, column(k), x_send.at[k - 1], x_recv.at[k - 1])
-
-    def bundle(step):
-        return 32 + (z + 16 + step) % 8 * 4
-
-    def along_z(step, t):
-        start = bundle(-step * t)
-        if t == 3:
-            start = start + (0 if step > 0 else 2)
+    def row(step):
+        return (z + 16 + step) % 8
+
+    def along_z(step, arrived=False):
+        ref = chunks.at[1, row(-step) if arrived else z, x]
+        return copy(ref, ref, plane(step), z_send.at[step % 8], z_recv.at[step % 8])
+
+    def along_x(n, k, arrived=False):
+        ref = chunks.at[1, row(n), (x + 4 - k) % 4 if arrived else x]
+        return copy(ref, ref, column(k), x_send.at[n % 8, k - 1], x_recv.at[n % 8, k - 1])
+
+    def along_r(step, n, arrived=False):
         side = 0 if step > 0 else 1
-        count = 2 if t == 3 else 4
-        return copy(start, count, start, plane(step), z_send.at[side, t], z_recv.at[side, t])
-
-    def arrived_z(step, t):
-        start = bundle(-step * (t + 1))
-        if t == 3:
-            start = start + (0 if step > 0 else 2)
-        side = 0 if step > 0 else 1
-        count = 2 if t == 3 else 4
-        return copy(start, count, start, plane(step), z_send.at[side, t], z_recv.at[side, t])
-
-    def along_r(step, k):
-        side = 0 if step > 0 else 1
-        to = bundle(k) + (-32 if step > 0 else 32)
-        return copy(bundle(k), 4, to, slab(step), r_send.at[side, k], r_recv.at[side, k])
-
-    def arrived_r(step, k):
-        side = 0 if step > 0 else 1
-        to = bundle(k) + (-32 if step > 0 else 32)
-        return copy(to, 4, to, slab(step), r_send.at[side, k], r_recv.at[side, k])
-
-    def give(k):
+        target = chunks.at[2 * side, row(n)]
+        source = target if arrived else chunks.at[1, row(n)]
+        return copy(source, target, slab(step), r_send.at[side, n % 8], r_recv.at[side, n % 8])
+
+    def spread(n):
+        for k in (2, 1, 3):
+            along_x(n, k).start()
+
+    def give(n):
+        for k in (1, 2, 3):
+            along_x(n, k, True).wait_recv()
         for step in (1, -1):
-            along_r(step, k % 8).start()
-
-    for k in (2, 1, 3):
-        along_x(k).start()
-    for k in (1, 2, 3):
-        begin = 32 + z * 4 + (x + 4 - k) % 4
-        copy(begin, 1, begin, column(k), x_send.at[k - 1], x_recv.at[k - 1]).wait_recv()
-    along_z(1, 0).start()
-    along_z(-1, 0).start()
+            along_r(step, n).start()
+
+    for step in STEPS:
+        along_z(step).start()
+    spread(0)
+    for step in (-1, 1):
+        along_z(-step, True).wait_recv()
+        spread(step)
     give(0)
-    for t in range(3):
+    for far in (2, 3, 4):
+        for step in (-far, far) if far < 4 else (4,):
+            along_z(-step if far < 4 else 4, True).wait_recv()
+            spread(step)
+        give(1 - far)
+        give(far - 1)
+    give(4)
+    for n in range(8):
         for step in (1, -1):
-            arrived_z(step, t).wait_recv()
-            along_z(step, t + 1).start()
-            give(-step * (t + 1))
-    arrived_z(1, 3).wait_recv()
-    arrived_z(-1, 3).wait_recv()
-    give(4)
-    for k in range(8):
-        arrived_r(1, k).wait_recv()
-        arrived_r(-1, k).wait_recv()
+            along_r(step, n, True).wait_recv()
     read_lists(chunks, lists, region, group)
-    for k in (1, 2, 3):
-        along_x(k).wait_send()
-    for t in range(4):
-        along_z(1, t).wait_send()
-        along_z(-1, t).wait_send()
-    for k in range(8):
-        along_r(1, k).wait_send()
-        along_r(-1, k).wait_send()
+    for step in STEPS:
+        along_z(step).wait_send()
+    for n in range(8):
+        for k in (1, 2, 3):
+            along_x(n, k).wait_send()
+        for step in (1, -1):
+            along_r(step, n).wait_send()
 
 
 def exchange_call(geom, density, velocity, pressure, live, pair):
     vmem = pl.BlockSpec(memory_space=pltpu.VMEM)
-    smem = pl.BlockSpec(memory_space=pltpu.SMEM)
+    def rows(v, first):
+        return jnp.pad(v, ((first, 12 - first - v.shape[0]), (0, 2 * BLOCK - v.shape[1])))
+
+    values = rows(geom, 0) + rows(density[None], 4) + rows(velocity, 5) + rows(pressure[None], 8)
+    values = values + rows(pair.T.astype(F32), 9) + rows(live[None].astype(F32), 11)
     dma = pltpu.SemaphoreType.DMA
-    return pl.pallas_call(
+    chunks, place, lists = pl.pallas_call(
         exchange,
         out_shape=(
-            jax.ShapeDtypeStruct((96, 40, 128), F32),
+            jax.ShapeDtypeStruct((LAYERS, 8, 4, 40, 128), F32),
             jax.ShapeDtypeStruct((8, 512), F32),
             jax.ShapeDtypeStruct((24, 128), jnp.int32),
         ),
-        in_specs=[vmem, vmem, vmem, vmem, smem, vmem],
+        in_specs=[vmem],
         out_specs=(vmem, vmem, vmem),
         scratch_shapes=[
             pltpu.VMEM((8, 128), F32),
-            dma((3,)),
-            dma((3,)),
-            dma((2, 4)),
-            dma((2, 4)),
+            dma((8,)),
+            dma((8,)),
+            dma((8, 3)),
+            dma((8, 3)),
             dma((2, 8)),
             dma((2, 8)),
         ],
@@ -214,7 +209,8 @@
             collective_id=0, has_side_effects=True, vmem_limit_bytes=16 * 1024 * 1024
         ),
         name="gather_sites",
-    )(geom, density[None], velocity, pressure[None], live, pair.T)
+    )(values)
+    return chunks.reshape(LAYERS * 32, 40, 128), place, lists
 
 
 def direction(step, wanted):

time: 66.2 us -> 59.6 us (0.900)
  Pallas kernels: 61.2 us -> 56.7 us
  local copies, waits for them, and re-layouts: 4.08 us -> 0 us
  other arithmetic: 0 us -> 2.1 us
    pallas_call x1, Pallas kernels: 35.5 us -> 31 us  [exchange_call(): pl.pallas_call(exchange, out_shape=(jax.ShapeDtypeStruct((LAYERS, 8, 4, 4...]
    unnamed x12 -> x0, local copies, waits for them, and re-layouts: 4.08 us -> none
    convert_element_type x0 -> x2, other arithmetic: none -> 1.34 us  [the longest x1 0.68 us: exchange_call(): pair.T.astype(F32)]
    add x0 -> x1, other arithmetic: none -> 0.76 us  [exchange_call(): values + rows(pair.T.astype(F32), 9) + rows(live[None].astype(F32), 11)]
where the time goes in v4:
time: 59.6 us; the launch traced here: 59.4 us
  Pallas kernels  56.7 us (95%)
  other arithmetic  2.1 us (4%)
  between operations  0.64 us (1%)
    pallas_call x1, Pallas kernels, exchange_call(): pl.pallas_call(exchange, out_shape=(jax.ShapeDtypeStruct((LAYERS, 8, 4, 4...  31 us
    pallas_call x1, Pallas kernels, sweep_call(): pl.pallas_call(sweep, out_shape=(jax.ShapeDtypeStruct((15, 512), F32), ja...  25.7 us

profile of v4, /device:TPU:25, one launch (start us, length us, event | category | flops | bytes accessed | tf_op | source)
XLA Modules:
  0.0 59.4 jit_solution(8531936306272948499)
XLA Ops:
  0.6 0.7 %convert_bitcast_fusion.1 = f32[1,2]{1,0:T(1,128)S(1)} fusion(s32[2]{0:T(128)} %param.10), kind=kLoop, calls=%fused_computation.2 | loop fusion | flops 2 | bytes 16 | tf_op jit(solution)/shard_map/convert_element_type | solution.py:188
  1.3 0.7 %convert_bitcast_fusion = f32[2,14]{1,0:T(2,128)S(1)} fusion(s32[14,2]{0,1:T(2,128)} %param.11), kind=kLoop, calls=%fused_computation.1 | loop fusion | flops 28 | bytes 224 | tf_op jit(solution)/shard_map/convert_element_type | solution.py:188
  2.0 0.8 %pad_add_fusion.values = f32[12,512]{1,0:T(8,128)S(1)} fusion(f32[1,2]{1,0:T(1,128)S(1)} %convert_bitcast_fusion.1, f32[2,14]{1,0:T(2,128)S(1)} %convert_bitcast_fusion, f32[1,512]{1,0:T(1,128)} %bitcast.10, f32[3,512]{1,0:T(4,128)} %param.8, f32[1,512]{1,0:T(1,128)} %bitcast.11, f32[4,512]{1,0:T(4,128)} %param.6), kind=kLoop, calls=%fused_computation | loop fusion | flops 30720 | bytes 43128 | tf_op jit(solution)/shard_map/add | solution.py:188
  2.7 31.0 %gather_sites.1 = (f32[3,8,4,40,128]{4,3,2,1,0:T(8,128)S(1)}, f32[8,512]{1,0:T(8,128)S(1)}, s32[24,128]{1,0:T(8,128)S(1)}) custom-call(f32[12,512]{1,0:T(8,128)S(1)} %pad_add_fusion.values), custom_call_target="tpu_custom_call" | custom-call | tf_op jit(solution)/shard_map/gather_sites/pallas_call | solution.py:190
  33.8 25.7 %sweep.1 = (f32[15,512]{1,0:T(8,128)}, f32[5,512]{1,0:T(8,128)}) custom-call(s32[3072]{0:T(1024)S(1)} %bitcast.9, f32[96,40,128]{2,1,0:T(8,128)S(1)} %bitcast.8, f32[8,512]{1,0:T(8,128)S(1)} %get-tuple-element.7.place), custom_call_target="tpu_custom_call" | custom-call | tf_op jit(solution)/shard_map/sweep/pallas_call | solution.py:613

commit v5 on v4

--- a/solution.py
+++ b/solution.py
@@ -16,7 +16,6 @@
 gamma = 5.0 / 3.0
 HEAD, TAIL, CORNER = 64, 78, 92
 MESH = pl.DeviceIdType.MESH
-SELF = 13
 
 
 def iota(shape, dim):
@@ -268,71 +267,96 @@
 
 
 def collect_sites(chunks, source, used, near):
-    group = iota((8, 128), 1) // 8
+    lanes = iota((8, 128), 1)
+    group = lanes // 8
     bit = [(group >> k) % 2 == 0 for k in range(4)]
-
-    def one_way(way, _):
-        @pl.when(used[way] > 0)
+    low_y, low_z, low_x = iota((8, 128), 0) < 4, lanes % 8 < 4, (group % 4) < 2
+
+    def choose(sides, mask, value):
+        if len(sides) == 1:
+            return value(sides[0])
+        return jnp.where(mask, value(2), value(0))
+
+    for kind in range(8):
+        xs, ys, zs = [(2, 0) if kind & b else (1,) for b in (4, 2, 1)]
+        ways = [(sx * 9 + sy * 3 + sz) for sx in xs for sy in ys for sz in zs]
+        any_used = sum(used[way] for way in ways)
+
+        @pl.when(any_used > 0)
         def _present():
-            froms = [source[way * 16 + p] for p in range(LIST)]
-            there = jnp.zeros((8, 128), jnp.int32)
-            second = jnp.zeros((8, 128), jnp.int32)
-            for p in range(LIST):
-                mask = group == p
-                there = jnp.where(mask, jnp.where(froms[p] >= 0, 1, 0), there)
-                second = jnp.where(mask, froms[p] & 1, second)
-            there, second = there > 0, second > 0
-            at = [jnp.maximum(f, 0) >> 1 for f in froms]
-            at += [at[0], at[1]]
+            froms = {(way, p): source[way * 16 + p] for way in ways for p in range(LIST)}
+
+            def code(way, p):
+                f = froms[way, p]
+                return jnp.where(f >= 0, 1 + 2 * (f & 1), 0)
+
+            codes = {}
+            for sx in xs:
+                codes[sx] = jnp.zeros((8, 128), jnp.int32)
+                for p in range(LIST):
+                    value = choose(
+                        ys,
+                        low_y,
+                        lambda sy: choose(zs, low_z, lambda sz: code(sx * 9 + sy * 3 + sz, p)),
+                    )
+                    codes[sx] = jnp.where(group == p, value, codes[sx])
+
+            def tile(p, rows):
+                def load(sx, sy, sz):
+                    return chunks[jnp.maximum(froms[sx * 9 + sy * 3 + sz, p], 0) >> 1, rows, :]
+
+                return choose(
+                    xs,
+                    low_x,
+                    lambda sx: choose(
+                        ys, low_y, lambda sy: choose(zs, low_z, lambda sz: load(sx, sy, sz))
+                    ),
+                )
+
             for t in range(5):
-                v = [chunks[at[p], 8 * t : 8 * t + 8, :] for p in range(16)]
+                v = [tile(p, slice(8 * t, 8 * t + 8)) for p in range(LIST)]
+                v += v[:2]
                 for k in (0, 1, 3):
                     step = 1 << k
                     for p in range(16):
                         if not p & step:
                             v[p], v[p + step] = swap(v[p], v[p + step], bit[k], 8 * step)
-                for n in range(8):
+                for n in range(8 if t < 4 else 4):
                     par, x = n // 4, n % 4
+                    info = codes[xs[0] if x < 2 else xs[-1]]
+                    second = info >= 2
                     low, high = v[8 * par + x], v[8 * par + x + 4]
                     low = jnp.where(second, pltpu.roll(low, 96, 1), low)
                     high = jnp.where(second, high, pltpu.roll(high, 32, 1))
-                    out = jnp.where(there, jnp.where(bit[2], low, high), 0.0)
-                    if 2 * t + par == 8:
-                        near[way, 9, x] = out
+                    out = jnp.where(info > 0, jnp.where(bit[2], low, high), 0.0)
+                    if t == 4:
+                        if kind == 0:
+                            near[0, 9, x] = out
                         out = jnp.where(out > 0.0, 1.0, 0.0)
-                    if 2 * t + par < 9:
-                        near[way, 2 * t + par, x] = out
-
-        @pl.when(used[way] == 0)
+                    near[kind, 2 * t + par, x] = out
+
+        @pl.when(any_used == 0)
         def _absent():
-            near[way] = jnp.zeros((10, 4, 8, 128), F32)
-
-        return _
-
-    lax.fori_loop(0, 27, one_way, 0)
-
-
-def shifted(base, below, above, z, dz):
+            near[kind] = jnp.zeros((10, 4, 8, 128), F32)
+
+
+def shifted(base, outer, z, dz):
     if dz == 0:
         return base
     inside = pltpu.roll(base, (-dz) % 128, 1)
     if dz > 0:
-        return jnp.where(z + dz < 8, inside, pltpu.roll(above, 8 - dz, 1))
-    return jnp.where(z + dz >= 0, inside, pltpu.roll(below, 128 - 8 - dz, 1))
+        return jnp.where(z + dz < 8, inside, pltpu.roll(outer, 8 - dz, 1))
+    return jnp.where(z + dz >= 0, inside, pltpu.roll(outer, 128 - 8 - dz, 1))
 
 
 def shift_sites(near, halo):
     z = iota((8, 128), 1) % 8
-    upper = iota((8, 128), 0) < 4
 
     def one_row(row, _):
         for xe in range(8):
-            sx, x = (0, xe + 2) if xe < 2 else (1, xe - 2) if xe < 6 else (2, xe - 6)
-            mid = [near[sx * 9 + 3 + sz, row, x] for sz in (1, 0, 2)]
-            rim = [
-                jnp.where(upper, near[sx * 9 + 6 + sz, row, x], near[sx * 9 + sz, row, x])
-                for sz in (1, 0, 2)
-            ]
+            mx, x = (4, xe + 2) if xe < 2 else (0, xe - 2) if xe < 6 else (4, xe - 6)
+            mid = near[mx, row, x], near[mx + 1, row, x]
+            rim = near[mx + 2, row, x], near[mx + 3, row, x]
             for dz in range(-2, 3):
                 halo[dz + 2, row, xe, 8:16, :] = shifted(*mid, z, dz)
                 edge = shifted(*rim, z, dz)
@@ -345,17 +369,16 @@
 
 def moments(near, halo, fields):
     def one_plane(x, _):
-        xi, yi, zi = [near[SELF, k, x] for k in range(3)]
-        qi = [near[SELF, 3 + k, x] for k in range(5)]
-        alive, radius = near[SELF, 8, x], near[SELF, 9, x]
+        xi, yi, zi = [near[0, k, x] for k in range(3)]
+        qi = [near[0, 3 + k, x] for k in range(5)]
+        alive, radius = near[0, 8, x], near[0, 9, x]
         radius = jnp.where(radius > 0.0, radius, 1.0)
         inverse_radius = 1.0 / radius
 
-        def step(n, sums):
-            dz = n // 5
-            xe = n % 5 + x
+        def step(dz, dx, steps, sums):
+            xe = dx + x
             sums = list(sums)
-            for dy in range(-2, 3):
+            for dy in steps:
                 near_j = [halo[dz, k, xe, 8 + dy : 16 + dy, :] for k in range(9)]
                 ox, oy, oz = near_j[0] - xi, near_j[1] - yi, near_j[2] - zi
                 square = ox * ox + oy * oy + oz * oz
@@ -372,7 +395,12 @@
             return tuple(sums)
 
         zero = jnp.zeros((8, 128), F32)
-        sums = lax.fori_loop(0, 25, step, (zero,) * 22)
+        every, inner = range(-2, 3), range(-1, 2)
+        sums = lax.fori_loop(
+            0, 15, lambda n, v: step(1 + n // 5, n % 5, every, v), (zero,) * 22
+        )
+        sums = lax.fori_loop(0, 6, lambda n, v: step(n // 3 * 4, 1 + n % 3, every, v), sums)
+        sums = lax.fori_loop(0, 4, lambda n, v: step(n // 2 * 4, n % 2 * 4, inner, v), sums)
         omega = sums[0] + (1.0 - alive)
         per = 1.0 / omega
         shift = ridge_scale * radius * radius
@@ -388,7 +416,7 @@
         ]
         over = 1.0 / (m[0] * c[0] + m[3] * c[3] + m[4] * c[4])
         b = [v * over for v in c]
-        rows = [xi, yi, zi] + qi + [near[SELF, 9, x]]
+        rows = [xi, yi, zi] + qi + [near[0, 9, x]]
         square = per * per
         rows += [v * square for v in b]
         for k in range(5):
@@ -399,7 +427,7 @@
         at = pl.ds(pl.multiple_of(x * 128, 128), 128)
         for k in range(15):
             pair = jnp.concatenate(rows[2 * k : 2 * k + 2], axis=0)
-            for n, part in enumerate(split3(pair)):
+            for n, part in enumerate(split3(pair)[: 3 if k < 2 else 2]):
                 fields[240 * n + 16 * k : 240 * n + 16 * k + 16, at] = part
         return _
 
@@ -411,34 +439,42 @@
     z = lanes % 8
     sources = iota((128, 128), 0)
 
-    def one_way(n, _):
-        sz = n // 3
-        sy = n % 3
-        any_used = face_used[sy * 3 + sz] + face_used[9 + sy * 3 + sz] + face_used[18 + sy * 3 + sz]
-
-        @pl.when(any_used > 0)
-        def _present():
-            hot = []
-            for x in range(4):
-                wanted = jnp.full((1, 128), -1, jnp.int32)
-                for sx, xe in ((1, x + 2), (2, x + 6) if x < 2 else (0, x - 2)):
-                    for s in range(2):
-                        p = faces[s * 28 + sx * 9 + sy * 3 + sz]
-                        lane = jnp.where(p >= 0, p * 8 + z, -1)
-                        wanted = jnp.where(lanes // 8 == xe * 2 + s, lane, wanted)
-                hot.append(jnp.where(sources == wanted, 1.0, 0.0).astype(BF16))
-            found = jnp.dot(
-                fields[...], jnp.concatenate(hot, axis=0), preferred_element_type=F32
-            )
-            around[n] = found[0:240] + found[240:480] + found[480:720]
-
-        @pl.when(any_used == 0)
-        def _absent():
-            around[n] = jnp.zeros((240, 128), F32)
-
-        return _
-
-    lax.fori_loop(0, 9, one_way, 0)
+    def hot(sy, zs):
+        blocks = []
+        for x in range(4):
+            wanted = jnp.full((1, 128), -1, jnp.int32)
+            for sx, xe in ((1, x + 2), (2, x + 6) if x < 2 else (0, x - 2)):
+                for s in range(2):
+                    p = [faces[s * 28 + sx * 9 + sy * 3 + sz] for sz in zs]
+                    p = p[0] if len(p) == 1 else jnp.where(z < 4, p[0], p[1])
+                    lane = jnp.where(p >= 0, p * 8 + z, -1)
+                    wanted = jnp.where(lanes // 8 == xe * 2 + s, lane, wanted)
+            blocks.append(jnp.where(sources == wanted, 1.0, 0.0).astype(BF16))
+        return jnp.concatenate(blocks, axis=0)
+
+    def pick(columns):
+        found = jnp.dot(
+            fields[...], jnp.concatenate(columns, axis=1), preferred_element_type=F32
+        )
+        first = found[0:32] + found[240:272] + found[480:512]
+        return jnp.concatenate([first, found[32:240] + found[272:480]], axis=0)
+
+    low_y = iota((240, 128), 0) % 8 < 4
+    found = pick([hot(1, (1,)), hot(1, (2, 0)), hot(0, (1,)), hot(2, (1,))])
+    around[0] = found[:, 0:128]
+    around[1] = found[:, 128:256]
+    around[2] = jnp.where(low_y, found[:, 384:512], found[:, 256:384])
+    corner = [face_used[sx * 9 + sy * 3 + sz] for sx in range(3) for sy in (0, 2) for sz in (0, 2)]
+    any_corner = sum(corner)
+
+    @pl.when(any_corner > 0)
+    def _present():
+        found = pick([hot(0, (2, 0)), hot(2, (2, 0))])
+        around[3] = jnp.where(low_y, found[:, 128:256], found[:, 0:128])
+
+    @pl.when(any_corner == 0)
+    def _absent():
+        around[3] = jnp.zeros((240, 128), F32)
 
 
 def shift_fields(around, wide, inner):
@@ -447,18 +483,13 @@
     outer = (lanes < 16) | (lanes >= 112)
     middle = (lanes >= 32) & (lanes < 96)
     left = lanes < 64
-    upper = iota((8, 128), 0) < 4
 
     def some_rows(n, _):
         for m in range(3):
             row = n * 3 + m
             at = pl.ds(pl.multiple_of(row * 8, 8), 8)
-            mid = [around[sz * 3 + 1, at, :] for sz in (1, 0, 2)]
-            rim = [
-                jnp.where(upper, around[sz * 3 + 2, at, :], around[sz * 3, at, :])
-                for sz in (1, 0, 2)
-            ]
-            for is_rim, parts in ((False, mid), (True, rim)):
+            for is_rim in (False, True):
+                parts = around[2 * is_rim, at, :], around[2 * is_rim + 1, at, :]
                 for dz in range(-2, 3):
                     far = shifted(*parts, z, dz)
                     half = pltpu.roll(far, 64, 1)
@@ -548,10 +579,10 @@
     def add(order, sums, far):
         return tuple(a + b for a, b in zip(sums, face(lambda row: inner[order, row], far)))
 
-    def step(dz, sums):
+    def step(dz, reach, sums):
         sums = list(sums)
         for k in range(2):
-            for dy in range(-2, 3):
+            for dy in range(-2, 3) if k else range(-reach, reach + 1):
                 sums[k] = add(k, sums[k], lambda row: wide[dz, k, row, 8 + dy : 16 + dy, :])
         for d in (-2, 1):
             sums[2] = add(
@@ -564,7 +595,8 @@
         return tuple(sums)
 
     zero = (jnp.zeros((8, 128), F32),) * 5
-    two, one, same = lax.fori_loop(0, 5, step, (zero, zero, zero))
+    sums = lax.fori_loop(1, 4, lambda dz, v: step(dz, 2, v), (zero, zero, zero))
+    two, one, same = lax.fori_loop(0, 2, lambda n, v: step(4 * n, 1, v), sums)
     for d in (0, 1):
         same = add(
             2,
@@ -620,10 +652,10 @@
             pltpu.SMEM((28,), jnp.int32),
             pltpu.SMEM((56,), jnp.int32),
             pltpu.SMEM((28,), jnp.int32),
-            pltpu.VMEM((27, 10, 4, 8, 128), F32),
+            pltpu.VMEM((8, 10, 4, 8, 128), F32),
             pltpu.VMEM((5, 9, 8, 24, 128), F32),
-            pltpu.VMEM((720, 512), BF16),
-            pltpu.VMEM((9, 240, 128), F32),
+            pltpu.VMEM((512, 512), BF16),
+            pltpu.VMEM((4, 240, 128), F32),
             pltpu.VMEM((5, 3, 30, 24, 128), F32),
             pltpu.VMEM((3, 30, 8, 128), F32),
         ],

time: 59.6 us -> 55.1 us (0.924)
  the two profiles are of different devices: /device:TPU:25 before, /device:TPU:1 now
where the time goes in v5:
time: 55.1 us; the launch traced here: 54.4 us
  Pallas kernels  51.7 us (94%)
  other arithmetic  2.1 us (4%)
  between operations  0.64 us (1%)
    pallas_call x1, Pallas kernels, exchange_call(): pl.pallas_call(exchange, out_shape=(jax.ShapeDtypeStruct((LAYERS, 8, 4, 4...  30.6 us
    pallas_call x1, Pallas kernels, sweep_call(): pl.pallas_call(sweep, out_shape=(jax.ShapeDtypeStruct((15, 512), F32), ja...  21.1 us

profile of v5, /device:TPU:1, one launch (start us, length us, event | category | flops | bytes accessed | tf_op | source)
XLA Modules:
  0.0 54.4 jit_solution(5225239356766672017)
XLA Ops:
  0.6 0.7 %convert_bitcast_fusion.1 = f32[1,2]{1,0:T(1,128)S(1)} fusion(s32[2]{0:T(128)} %param.10), kind=kLoop, calls=%fused_computation.2 | loop fusion | flops 2 | bytes 16 | tf_op jit(solution)/shard_map/convert_element_type | solution.py:187
  1.3 0.7 %convert_bitcast_fusion = f32[2,14]{1,0:T(2,128)S(1)} fusion(s32[14,2]{0,1:T(2,128)} %param.11), kind=kLoop, calls=%fused_computation.1 | loop fusion | flops 28 | bytes 224 | tf_op jit(solution)/shard_map/convert_element_type | solution.py:187
  2.0 0.8 %pad_add_fusion.values = f32[12,512]{1,0:T(8,128)S(1)} fusion(f32[1,2]{1,0:T(1,128)S(1)} %convert_bitcast_fusion.1, f32[2,14]{1,0:T(2,128)S(1)} %convert_bitcast_fusion, f32[1,512]{1,0:T(1,128)} %bitcast.10, f32[3,512]{1,0:T(4,128)} %param.8, f32[1,512]{1,0:T(1,128)} %bitcast.11, f32[4,512]{1,0:T(4,128)} %param.6), kind=kLoop, calls=%fused_computation | loop fusion | flops 30720 | bytes 43128 | tf_op jit(solution)/shard_map/add | solution.py:187
  2.7 30.6 %gather_sites.1 = (f32[3,8,4,40,128]{4,3,2,1,0:T(8,128)S(1)}, f32[8,512]{1,0:T(8,128)S(1)}, s32[24,128]{1,0:T(8,128)S(1)}) custom-call(f32[12,512]{1,0:T(8,128)S(1)} %pad_add_fusion.values), custom_call_target="tpu_custom_call" | custom-call | tf_op jit(solution)/shard_map/gather_sites/pallas_call | solution.py:189
  33.3 21.1 %sweep.1 = (f32[15,512]{1,0:T(8,128)}, f32[5,512]{1,0:T(8,128)}) custom-call(s32[3072]{0:T(1024)S(1)} %bitcast.9, f32[96,40,128]{2,1,0:T(8,128)S(1)} %bitcast.8, f32[8,512]{1,0:T(8,128)S(1)} %get-tuple-element.7.place), custom_call_target="tpu_custom_call" | custom-call | tf_op jit(solution)/shard_map/sweep/pallas_call | solution.py:645

commit v6 on v5

--- a/solution.py
+++ b/solution.py
@@ -30,13 +30,25 @@
     return high, middle, low
 
 
-def prepare(values, line, place):
+def order_key(heads, index):
+    parity = (heads - 2.0 * jnp.floor(heads * 0.5)).astype(jnp.int32)
+    return jnp.where((heads >= 0.0) & (index < LIST), parity, 2)
+
+
+def prepare(values, place):
     lanes = iota((1, 128), 1)
     total = jnp.zeros((40, 128), F32)
-    line[...] = jnp.zeros((8, 128), F32)
-    line[0:1, HEAD : HEAD + LIST] = values[9:10, 0:LIST]
-    line[0:1, TAIL : TAIL + LIST] = values[10:11, 0:LIST]
-    listed = line[0:1, :]
+    both = jnp.concatenate([values[8:12, 0:128], values[8:12, 0:128]], axis=0).T[0:16]
+    kinds = [order_key(values[9:10, 0:128], lanes), order_key(both[:, 1:2], iota((16, 1), 0))]
+    here, there = iota((16, 128), 1), iota((16, 128), 0)
+    ahead = (kinds[0] < kinds[1]) | ((kinds[0] == kinds[1]) & (here < there))
+    ahead = jnp.where(ahead & (here < LIST), 1.0, 0.0)
+    rank = jnp.sum(ahead, axis=1, keepdims=True).astype(jnp.int32)
+    listed = jnp.where((here == TAIL + rank) & (there < LIST), both[:, 2:3], 0.0)
+    listed = jnp.sum(listed, axis=0, keepdims=True)
+    for s in range(2):
+        count = jnp.sum(jnp.where(kinds[0] == s, 1.0, 0.0), axis=1, keepdims=True)
+        listed = listed + jnp.where(lanes == HEAD + s, count, 0.0)
     for s in range(2):
         at = slice(s * BLOCK, (s + 1) * BLOCK)
         corner = values[0:4, at]
@@ -81,7 +93,7 @@
         rows = chunks[:, :, m, 32, :].reshape(24, 128)
         steps = jnp.floor((rows - own) * scale + 0.5) * weight
         steps = steps + pltpu.roll(steps, 127, 1) + pltpu.roll(steps, 126, 1)
-        ids = jnp.where(rows < 0.0, -1.0, rows - first)
+        ids = jnp.where(lanes < TAIL, rows, rows - first)
         rows = jnp.where(lanes < CORNER, ids, steps).astype(jnp.int32)
         rows = jnp.where(lanes == CORNER + 1, region, jnp.where(lanes == CORNER + 2, group, rows))
         whole = jnp.where(lanes // 32 == m, pltpu.roll(rows, (64 + 32 * m) % 128, 1), whole)
@@ -92,7 +104,7 @@
 
 
 def exchange(
-    values, chunks, place, lists, line,
+    values, chunks, place, lists,
     z_send, z_recv, x_send, x_recv, r_send, r_recv,
 ):
     region, group = lax.axis_index("region"), lax.axis_index("group")
@@ -111,7 +123,7 @@
     barrier = pltpu.get_barrier_semaphore()
     for partner in partners:
         pl.semaphore_signal(barrier, inc=1, device_id=partner, device_id_type=MESH)
-    chunks[1, z, x] = prepare(values, line, place)
+    chunks[1, z, x] = prepare(values, place)
     pl.semaphore_wait(barrier, len(partners))
 
     def copy(source, target, device, send, recv):
@@ -196,7 +208,6 @@
         in_specs=[vmem],
         out_specs=(vmem, vmem, vmem),
         scratch_shapes=[
-            pltpu.VMEM((8, 128), F32),
             dma((8,)),
             dma((8,)),
             dma((8, 3)),
@@ -240,21 +251,36 @@
         return lists[(block >> 1) * 32 + 28 + 3 * (block & 1)]
 
     def slot(p, _):
-        head = lists[own + p]
-        listed = head >= 0
+        first, second = lists[own], lists[own + 1]
+        listed = p < first + second
+        odd = jnp.where(p < first, 0, 1)
         tail = jnp.where(listed, lists[own + LIST + p], 64)
         place = code(tail)
-        way = direction(place - lists[own + 28 + 3 * (head & 1)], listed)
-        faces[(head & 1) * 28 + way] = p
+        way = direction(place - lists[own + 28 + 3 * odd], listed)
+        faces[odd * 28 + way] = p
         face_used[way] = 1
         at = (tail >> 1) * 32
-        for k in range(LIST):
-            there = lists[at + LIST + k]
-            near = listed & (lists[at + k] == tail) & (there >= 0) & (there < 192)
+        other = tail & 1
+        count = jnp.where(listed, jnp.where(other == 0, lists[at], lists[at + 1]), 0)
+        start = at + LIST + jnp.where(other == 0, 0, lists[at])
+
+        def entry(k):
+            near = k < count
+            there = lists[jnp.where(near, start + k, at)]
+            near = near & (there >= 0) & (there < 192)
             there = jnp.where(near, there, 0)
             towards = direction(code(there) - place, near)
             source[towards * 16 + p] = there
             used[towards] = 1
+
+        for k in range(LIST // 2):
+            entry(k)
+
+        @pl.when(count > LIST // 2)
+        def _more():
+            for k in range(LIST // 2, LIST):
+                entry(k)
+
         return _
 
     lax.fori_loop(0, LIST, slot, 0)
@@ -313,15 +339,15 @@
                     ),
                 )
 
-            for t in range(5):
-                v = [tile(p, slice(8 * t, 8 * t + 8)) for p in range(LIST)]
+            def one_tile(t, _):
+                v = [tile(p, pl.ds(t * 8, 8)) for p in range(LIST)]
                 v += v[:2]
                 for k in (0, 1, 3):
                     step = 1 << k
                     for p in range(16):
                         if not p & step:
                             v[p], v[p + step] = swap(v[p], v[p + step], bit[k], 8 * step)
-                for n in range(8 if t < 4 else 4):
+                for n in range(8):
                     par, x = n // 4, n % 4
                     info = codes[xs[0] if x < 2 else xs[-1]]
                     second = info >= 2
@@ -329,11 +355,18 @@
                     low = jnp.where(second, pltpu.roll(low, 96, 1), low)
                     high = jnp.where(second, high, pltpu.roll(high, 32, 1))
                     out = jnp.where(info > 0, jnp.where(bit[2], low, high), 0.0)
-                    if t == 4:
-                        if kind == 0:
-                            near[0, 9, x] = out
-                        out = jnp.where(out > 0.0, 1.0, 0.0)
                     near[kind, 2 * t + par, x] = out
+                return _
+
+            if kind in (0, 1, 2, 4):
+                for t in range(5):
+                    one_tile(t, 0)
+            else:
+                lax.fori_loop(0, 5, one_tile, 0)
+            for x in range(4):
+                radius = near[kind, 8, x]
+                near[kind, 9, x] = radius
+                near[kind, 8, x] = jnp.where(radius > 0.0, 1.0, 0.0)
 
         @pl.when(any_used == 0)
         def _absent():
@@ -349,6 +382,15 @@
     return jnp.where(z + dz >= 0, inside, pltpu.roll(outer, 128 - 8 - dz, 1))
 
 
+def rim_rows(dy):
+    row = iota((8, 128), 0)
+    return row < dy if dy > 0 else row >= 8 + dy
+
+
+def across(dy, edge, middle):
+    return middle if dy == 0 else jnp.where(rim_rows(dy), edge, middle)
+
+
 def shift_sites(near, halo):
     z = iota((8, 128), 1) % 8
 
@@ -358,49 +400,61 @@
             mid = near[mx, row, x], near[mx + 1, row, x]
             rim = near[mx + 2, row, x], near[mx + 3, row, x]
             for dz in range(-2, 3):
-                halo[dz + 2, row, xe, 8:16, :] = shifted(*mid, z, dz)
-                edge = shifted(*rim, z, dz)
-                halo[dz + 2, row, xe, 0:8, :] = edge
-                halo[dz + 2, row, xe, 16:24, :] = edge
+                middle, edge = shifted(*mid, z, dz), shifted(*rim, z, dz)
+                for dy in range(-2, 3):
+                    halo[dz + 2, dy + 2, row, xe] = across(dy, edge, middle)
         return _
 
-    lax.fori_loop(0, 9, one_row, 0)
-
-
-def moments(near, halo, fields):
+    lax.fori_loop(0, 9, one_row, 0, unroll=3)
+
+
+def moments(near, halo, fields, spin, turn):
     def one_plane(x, _):
         xi, yi, zi = [near[0, k, x] for k in range(3)]
         qi = [near[0, 3 + k, x] for k in range(5)]
         alive, radius = near[0, 8, x], near[0, 9, x]
         radius = jnp.where(radius > 0.0, radius, 1.0)
-        inverse_radius = 1.0 / radius
-
-        def step(dz, dx, steps, sums):
-            xe = dx + x
-            sums = list(sums)
-            for dy in steps:
-                near_j = [halo[dz, k, xe, 8 + dy : 16 + dy, :] for k in range(9)]
-                ox, oy, oz = near_j[0] - xi, near_j[1] - yi, near_j[2] - zi
-                square = ox * ox + oy * oy + oz * oz
-                scaled = square * lax.rsqrt(jnp.maximum(square, 1e-12)) * inverse_radius
-                remain = jnp.maximum(1.0 - scaled, 0.0)
-                remain = remain * remain
-                w = remain * remain * (1.0 + 4.0 * scaled) * near_j[8]
-                wx, wy, wz = w * ox, w * oy, w * oz
-                terms = [w, wx * ox, wy * oy, wz * oz, wx * oy, wx * oz, wy * oz]
-                for k in range(5):
-                    change = near_j[3 + k] - qi[k]
-                    terms += [wx * change, wy * change, wz * change]
-                sums = [a + b for a, b in zip(sums, terms)]
-            return tuple(sums)
-
-        zero = jnp.zeros((8, 128), F32)
-        every, inner = range(-2, 3), range(-1, 2)
-        sums = lax.fori_loop(
-            0, 15, lambda n, v: step(1 + n // 5, n % 5, every, v), (zero,) * 22
-        )
-        sums = lax.fori_loop(0, 6, lambda n, v: step(n // 3 * 4, 1 + n % 3, every, v), sums)
-        sums = lax.fori_loop(0, 4, lambda n, v: step(n // 2 * 4, n % 2 * 4, inner, v), sums)
+        for k, value in enumerate([xi, yi, zi] + qi + [1.0 / radius]):
+            spin[k, 0:8, :] = value
+            spin[k, 8:16, :] = value
+        sums = [jnp.zeros((8, 128), F32)] * 22
+        for dy in range(-2, 3):
+            own = [spin[k, -dy % 8 : -dy % 8 + 8, :] for k in range(9)]
+
+            def step(dz, steps, total):
+                total = list(total)
+                for dx in steps:
+                    part = [halo[dz, dy + 2, k, x + dx] for k in range(9)]
+                    ox, oy, oz = [part[k] - own[k] for k in range(3)]
+                    square = ox * ox + oy * oy + oz * oz
+                    scaled = square * lax.rsqrt(jnp.maximum(square, 1e-12)) * own[8]
+                    remain = jnp.maximum(1.0 - scaled, 0.0)
+                    remain = remain * remain
+                    w = remain * remain * (1.0 + 4.0 * scaled) * part[8]
+                    wx, wy, wz = w * ox, w * oy, w * oz
+                    total[0] = total[0] + w
+                    total[1] = total[1] + wx * ox
+                    total[2] = total[2] + wy * oy
+                    total[3] = total[3] + wz * oz
+                    total[4] = total[4] + wx * oy
+                    total[5] = total[5] + wx * oz
+                    total[6] = total[6] + wy * oz
+                    for k in range(5):
+                        change = part[3 + k] - own[3 + k]
+                        for c, v in enumerate((wx, wy, wz)):
+                            total[7 + 3 * k + c] = total[7 + 3 * k + c] + v * change
+                return tuple(total)
+
+            total = (jnp.zeros((8, 128), F32),) * 22
+            wide = range(5) if abs(dy) < 2 else range(1, 4)
+            for dz in range(5):
+                total = step(dz, range(5) if dz in (1, 2, 3) else wide, total)
+            if dy != 0:
+                for k in range(22):
+                    turn[k, 0:8, :] = total[k]
+                    turn[k, 8:16, :] = total[k]
+                total = [turn[k, dy % 8 : dy % 8 + 8, :] for k in range(22)]
+            sums = [a + b for a, b in zip(sums, total)]
         omega = sums[0] + (1.0 - alive)
         per = 1.0 / omega
         shift = ridge_scale * radius * radius
@@ -477,6 +531,11 @@
         around[3] = jnp.zeros((240, 128), F32)
 
 
+HALF = 6
+TILES = [(0, -2, -2), (0, -1, -1), (0, 0, 0), (1, -2, -2), (1, -1, -1), (2, -2, -1)]
+TILES += [(0, 2, 2), (0, 1, 1), (1, 0, 0), (1, 2, 2), (1, 1, 1), (2, 1, 2), (2, 0, 0)]
+
+
 def shift_fields(around, wide, inner):
     lanes = iota((8, 128), 1)
     z = lanes % 8
@@ -488,24 +547,27 @@
         for m in range(3):
             row = n * 3 + m
             at = pl.ds(pl.multiple_of(row * 8, 8), 8)
-            for is_rim in (False, True):
-                parts = around[2 * is_rim, at, :], around[2 * is_rim + 1, at, :]
-                for dz in range(-2, 3):
-                    far = shifted(*parts, z, dz)
+            parts = [(around[n, at, :], around[n + 1, at, :]) for n in (0, 2)]
+            for dz in range(-2, 3):
+                orders = []
+                for base, beyond in parts:
+                    far = shifted(base, beyond, z, dz)
                     half = pltpu.roll(far, 64, 1)
-                    orders = far, jnp.where(outer, half, far), jnp.where(middle, far, half)
-                    for k, value in enumerate(orders):
-                        if is_rim:
-                            wide[dz + 2, k, row, 0:8, :] = value
-                            wide[dz + 2, k, row, 16:24, :] = value
-                        else:
-                            wide[dz + 2, k, row, 8:16, :] = value
-                    if dz == 0 and not is_rim:
-                        own = orders[2]
-                        back, on = pltpu.roll(own, 112, 1), pltpu.roll(own, 16, 1)
-                        inner[0, row] = pltpu.roll(own, 32, 1)
-                        inner[1, row] = jnp.where(left, back, on)
-                        inner[2, row] = own
+                    orders.append(
+                        (far, jnp.where(outer, half, far), jnp.where(middle, far, half))
+                    )
+                for tile, (k, first, second) in enumerate(TILES):
+                    value = across(first, orders[1][k], orders[0][k])
+                    if first != second:
+                        value = jnp.where(left, value, across(second, orders[1][k], orders[0][k]))
+                    wide[dz + 2, tile, row] = value
+                if dz == 0:
+                    own = orders[0][2]
+                    back, on = pltpu.roll(own, 112, 1), pltpu.roll(own, 16, 1)
+                    values = pltpu.roll(own, 32, 1), jnp.where(left, back, on), own
+                    for k, value in enumerate(values):
+                        inner[k, row, 0:8, :] = value
+                        inner[k, row, 8:16, :] = value
         return _
 
     lax.fori_loop(0, 10, some_rows, 0)
@@ -573,57 +635,72 @@
     return [jnp.where(live, t * area, 0.0) for t in terms + [heat]]
 
 
-def fluxes(wide, inner):
+def fluxes(wide, inner, turned, gains):
     left = iota((8, 128), 1) < 64
-
-    def add(order, sums, far):
-        return tuple(a + b for a, b in zip(sums, face(lambda row: inner[order, row], far)))
-
-    def step(dz, reach, sums):
-        sums = list(sums)
-        for k in range(2):
-            for dy in range(-2, 3) if k else range(-reach, reach + 1):
-                sums[k] = add(k, sums[k], lambda row: wide[dz, k, row, 8 + dy : 16 + dy, :])
-        for d in (-2, 1):
-            sums[2] = add(
-                2,
-                sums[2],
-                lambda row: jnp.where(
-                    left, wide[dz, 2, row, 8 + d : 16 + d, :], wide[dz, 2, row, 9 + d : 17 + d, :]
-                ),
+    zero = jnp.zeros((8, 128), F32)
+
+    def halves(first, second, load):
+        return load(first) if first == second else jnp.where(left, load(first), load(second))
+
+    def turn(row, _):
+        for n, (k, first, second) in enumerate(TILES):
+            turned[n, row] = halves(
+                first, second, lambda dy: inner[k, row, -dy % 8 : -dy % 8 + 8, :]
             )
-        return tuple(sums)
-
-    zero = (jnp.zeros((8, 128), F32),) * 5
-    sums = lax.fori_loop(1, 4, lambda dz, v: step(dz, 2, v), (zero, zero, zero))
-    two, one, same = lax.fori_loop(0, 2, lambda n, v: step(4 * n, 1, v), sums)
+        return _
+
+    lax.fori_loop(0, 30, turn, 0, unroll=10)
+    def add(sums, n, far):
+        return [a + b for a, b in zip(sums, face(lambda row: turned[n, row], far))]
+
+    def keep(sums, n):
+        for c, value in enumerate(sums):
+            gains[n, c, 0:8, :] = value
+
+    def some_tiles(part, _):
+        for m in range(HALF):
+            n = part * HALF + m
+            sums = [zero] * 5
+            for dz in range(1, 4) if m == 0 else range(5):
+                sums = add(sums, n, lambda row: wide[dz, n, row])
+            keep(sums, n)
+        return _
+
+    lax.fori_loop(0, 2, some_tiles, 0)
+    last = len(TILES) - 1
+    sums = [zero] * 5
     for d in (0, 1):
-        same = add(
-            2,
-            same,
-            lambda row: jnp.where(left, wide[d, 2, row, 8:16, :], wide[4 - d, 2, row, 8:16, :]),
+        sums = add(
+            sums, last, lambda row: jnp.where(left, wide[d, last, row], wide[4 - d, last, row])
         )
+    keep(sums, last)
     found = []
-    for a, b, c in zip(two, one, same):
-        total = c + pltpu.roll(a, 32, 1)
-        total = total + pltpu.roll(jnp.where(left, b, 0.0), 16, 1)
-        total = total + pltpu.roll(jnp.where(left, 0.0, b), 112, 1)
+    for c in range(5):
+        orders = [zero, zero, zero]
+        for n, (k, first, second) in enumerate(TILES):
+            gains[n, c, 8:16, :] = gains[n, c, 0:8, :]
+            part = halves(first, second, lambda dy: gains[n, c, dy % 8 : dy % 8 + 8, :])
+            orders[k] = orders[k] + part
+        two, one, same = orders
+        total = same + pltpu.roll(two, 32, 1)
+        total = total + pltpu.roll(jnp.where(left, one, 0.0), 16, 1)
+        total = total + pltpu.roll(jnp.where(left, 0.0, one), 112, 1)
         found.append(-(total + pltpu.roll(total, 64, 1)))
     return found
 
 
 def sweep(
     lists, chunks, place, gradients, rate, source, used, faces, face_used, near, halo, fields,
-    around, wide, inner,
+    around, wide, inner, spin, turn, turned, gains,
 ):
     fill_tables(lists, source, used, faces, face_used)
     collect_sites(chunks, source, used, near)
     shift_sites(near, halo)
-    moments(near, halo, fields)
+    moments(near, halo, fields, spin, turn)
     gather_fields(fields, faces, face_used, around)
     shift_fields(around, wide, inner)
-    rates = fluxes(wide, inner)
-    rows = [wide[2, 0, 15 + k, 8:16, :] for k in range(15)] + rates
+    rates = fluxes(wide, inner, turned, gains)
+    rows = [wide[2, 2, 15 + k] for k in range(15)] + rates
     found = jnp.concatenate(rows, axis=0)
     lane = place[1:2, :].astype(jnp.int32) + 32
     hot = jnp.where(iota((128, 512), 0) == lane, 1.0, 0.0).astype(BF16)
@@ -653,11 +730,15 @@
             pltpu.SMEM((56,), jnp.int32),
             pltpu.SMEM((28,), jnp.int32),
             pltpu.VMEM((8, 10, 4, 8, 128), F32),
-            pltpu.VMEM((5, 9, 8, 24, 128), F32),
+            pltpu.VMEM((5, 5, 9, 8, 8, 128), F32),
             pltpu.VMEM((512, 512), BF16),
             pltpu.VMEM((4, 240, 128), F32),
-            pltpu.VMEM((5, 3, 30, 24, 128), F32),
-            pltpu.VMEM((3, 30, 8, 128), F32),
+            pltpu.VMEM((5, len(TILES), 30, 8, 128), F32),
+            pltpu.VMEM((3, 30, 16, 128), F32),
+            pltpu.VMEM((9, 16, 128), F32),
+            pltpu.VMEM((22, 16, 128), F32),
+            pltpu.VMEM((len(TILES), 30, 8, 128), F32),
+            pltpu.VMEM((len(TILES), 5, 16, 128), F32),
         ],
         compiler_params=pltpu.CompilerParams(vmem_limit_bytes=48 * 1024 * 1024),
         name="sweep",

time: 55.1 us -> 51.6 us (0.936)
  Pallas kernels: 51.7 us -> 48.2 us
    pallas_call x1, Pallas kernels: 21.1 us -> 17.7 us  [sweep_call(): pl.pallas_call(sweep, out_shape=(jax.ShapeDtypeStruct((15, 512), F32), ja...]
where the time goes in v6:
time: 51.6 us; the launch traced here: 51 us
  Pallas kernels  48.2 us (93%)
  other arithmetic  2.1 us (4%)
  between operations  0.64 us (1%)
    pallas_call x1, Pallas kernels, exchange_call(): pl.pallas_call(exchange, out_shape=(jax.ShapeDtypeStruct((LAYERS, 8, 4, 4...  30.6 us
    pallas_call x1, Pallas kernels, sweep_call(): pl.pallas_call(sweep, out_shape=(jax.ShapeDtypeStruct((15, 512), F32), ja...  17.7 us

profile of v6, /device:TPU:1, one launch (start us, length us, event | category | flops | bytes accessed | tf_op | source)
XLA Modules:
  0.0 51.0 jit_solution(4781141798329579572)
XLA Ops:
  0.6 0.7 %convert_bitcast_fusion.1 = f32[1,2]{1,0:T(1,128)S(1)} fusion(s32[2]{0:T(128)} %param.10), kind=kLoop, calls=%fused_computation.2 | loop fusion | flops 2 | bytes 16 | tf_op jit(solution)/shard_map/convert_element_type | solution.py:199
  1.3 0.7 %convert_bitcast_fusion = f32[2,14]{1,0:T(2,128)S(1)} fusion(s32[14,2]{0,1:T(2,128)} %param.11), kind=kLoop, calls=%fused_computation.1 | loop fusion | flops 28 | bytes 224 | tf_op jit(solution)/shard_map/convert_element_type | solution.py:199
  2.0 0.8 %pad_add_fusion.values = f32[12,512]{1,0:T(8,128)S(1)} fusion(f32[1,2]{1,0:T(1,128)S(1)} %convert_bitcast_fusion.1, f32[2,14]{1,0:T(2,128)S(1)} %convert_bitcast_fusion, f32[1,512]{1,0:T(1,128)} %bitcast.10, f32[3,512]{1,0:T(4,128)} %param.8, f32[1,512]{1,0:T(1,128)} %bitcast.11, f32[4,512]{1,0:T(4,128)} %param.6), kind=kLoop, calls=%fused_computation | loop fusion | flops 30720 | bytes 43128 | tf_op jit(solution)/shard_map/add | solution.py:199
  2.7 30.6 %gather_sites.1 = (f32[3,8,4,40,128]{4,3,2,1,0:T(8,128)S(1)}, f32[8,512]{1,0:T(8,128)S(1)}, s32[24,128]{1,0:T(8,128)S(1)}) custom-call(f32[12,512]{1,0:T(8,128)S(1)} %pad_add_fusion.values), custom_call_target="tpu_custom_call" | custom-call | tf_op jit(solution)/shard_map/gather_sites/pallas_call | solution.py:201
  33.3 17.7 %sweep.1 = (f32[15,512]{1,0:T(8,128)}, f32[5,512]{1,0:T(8,128)}) custom-call(s32[3072]{0:T(1024)S(1)} %bitcast.9, f32[96,40,128]{2,1,0:T(8,128)S(1)} %bitcast.8, f32[8,512]{1,0:T(8,128)S(1)} %get-tuple-element.7.place), custom_call_target="tpu_custom_call" | custom-call | tf_op jit(solution)/shard_map/sweep/pallas_call | solution.py:722

commit v7 on v6

--- a/solution.py
+++ b/solution.py
@@ -174,8 +174,11 @@
         for step in (-far, far) if far < 4 else (4,):
             along_z(-step if far < 4 else 4, True).wait_recv()
             spread(step)
-        give(1 - far)
-        give(far - 1)
+        if far > 2:
+            give(2 - far)
+            give(far - 2)
+    give(-3)
+    give(3)
     give(4)
     for n in range(8):
         for step in (1, -1):
@@ -196,7 +199,7 @@
         return jnp.pad(v, ((first, 12 - first - v.shape[0]), (0, 2 * BLOCK - v.shape[1])))
 
     values = rows(geom, 0) + rows(density[None], 4) + rows(velocity, 5) + rows(pressure[None], 8)
-    values = values + rows(pair.T.astype(F32), 9) + rows(live[None].astype(F32), 11)
+    values = values + (rows(pair.T, 9) + rows(live[None], 11)).astype(F32)
     dma = pltpu.SemaphoreType.DMA
     chunks, place, lists = pl.pallas_call(
         exchange,

time: 51.6 us -> 49.3 us (0.955)
  other arithmetic: 2.1 us -> 0.8 us
    convert_element_type x2 -> x0, other arithmetic: 1.34 us -> none  [the longest x1 0.68 us: exchange_call(): pair.T.astype(F32)]
    pallas_call x1, Pallas kernels: 30.6 us -> 30 us  [exchange_call(): pl.pallas_call(exchange, out_shape=(jax.ShapeDtypeStruct((LAYERS, 8, 4, 4...]
where the time goes in v7:
time: 49.3 us; the launch traced here: 49.1 us
  Pallas kernels  47.7 us (97%)
  other arithmetic  0.8 us (2%)
  between operations  0.64 us (1%)
    pallas_call x1, Pallas kernels, exchange_call(): pl.pallas_call(exchange, out_shape=(jax.ShapeDtypeStruct((LAYERS, 8, 4, 4...  30 us
    pallas_call x1, Pallas kernels, sweep_call(): pl.pallas_call(sweep, out_shape=(jax.ShapeDtypeStruct((15, 512), F32), ja...  17.6 us

profile of v7, /device:TPU:1, one launch (start us, length us, event | category | flops | bytes accessed | tf_op | source)
XLA Modules:
  0.0 49.1 jit_solution(1940340910682922803)
XLA Ops:
  0.6 0.8 %convert_add_fusion.values = f32[12,512]{1,0:T(8,128)S(1)} fusion(s32[1,2]{1,0:T(1,128)} %bitcast.11, s32[2,14]{1,0:T(2,128)} %bitcast.10, f32[1,512]{1,0:T(1,128)} %bitcast.8, f32[3,512]{1,0:T(4,128)} %param.8, f32[1,512]{1,0:T(1,128)} %bitcast.9, f32[4,512]{1,0:T(4,128)} %param.6), kind=kLoop, calls=%fused_computation | loop fusion | flops 36864 | bytes 43128 | tf_op jit(solution)/shard_map/add | solution.py:202
  1.4 30.0 %gather_sites.1 = (f32[3,8,4,40,128]{4,3,2,1,0:T(8,128)S(1)}, f32[8,512]{1,0:T(8,128)S(1)}, s32[24,128]{1,0:T(8,128)S(1)}) custom-call(f32[12,512]{1,0:T(8,128)S(1)} %convert_add_fusion.values), custom_call_target="tpu_custom_call" | custom-call | tf_op jit(solution)/shard_map/gather_sites/pallas_call | solution.py:204
  31.5 17.6 %sweep.1 = (f32[15,512]{1,0:T(8,128)}, f32[5,512]{1,0:T(8,128)}) custom-call(s32[3072]{0:T(1024)S(1)} %bitcast.7, f32[96,40,128]{2,1,0:T(8,128)S(1)} %bitcast.6, f32[8,512]{1,0:T(8,128)S(1)} %get-tuple-element.7.place), custom_call_target="tpu_custom_call" | custom-call | tf_op jit(solution)/shard_map/sweep/pallas_call | solution.py:725

commit v8 on v7

--- a/solution.py
+++ b/solution.py
@@ -253,40 +253,48 @@
     def code(block):
         return lists[(block >> 1) * 32 + 28 + 3 * (block & 1)]
 
-    def slot(p, _):
-        first, second = lists[own], lists[own + 1]
-        listed = p < first + second
+    first = lists[own]
+    listed_rows = first + lists[own + 1]
+
+    def origin(p):
+        listed = p < listed_rows
         odd = jnp.where(p < first, 0, 1)
         tail = jnp.where(listed, lists[own + LIST + p], 64)
-        place = code(tail)
-        way = direction(place - lists[own + 28 + 3 * odd], listed)
-        faces[odd * 28 + way] = p
-        face_used[way] = 1
         at = (tail >> 1) * 32
         other = tail & 1
         count = jnp.where(listed, jnp.where(other == 0, lists[at], lists[at + 1]), 0)
         start = at + LIST + jnp.where(other == 0, 0, lists[at])
-
-        def entry(k):
-            near = k < count
-            there = lists[jnp.where(near, start + k, at)]
-            near = near & (there >= 0) & (there < 192)
-            there = jnp.where(near, there, 0)
-            towards = direction(code(there) - place, near)
-            source[towards * 16 + p] = there
-            used[towards] = 1
-
+        return listed, odd, at, count, start, code(tail)
+
+    def enter(p, k, at, count, start, place):
+        near = k < count
+        there = lists[jnp.where(near, start + k, at)]
+        near = near & (there >= 0) & (there < 192)
+        there = jnp.where(near, there, 0)
+        towards = direction(code(there) - place, near)
+        source[towards * 16 + p] = there
+        used[towards] = 1
+
+    def slot(p, most):
+        listed, odd, at, count, start, place = origin(p)
+        way = direction(place - lists[own + 28 + 3 * odd], listed)
+        faces[odd * 28 + way] = p
+        face_used[way] = 1
         for k in range(LIST // 2):
-            entry(k)
-
-        @pl.when(count > LIST // 2)
-        def _more():
+            enter(p, k, at, count, start, place)
+        return jnp.maximum(most, count)
+
+    most = lax.fori_loop(0, LIST, slot, 0, unroll=7)
+
+    @pl.when(most > LIST // 2)
+    def _more():
+        def rest(p, _):
+            listed, odd, at, count, start, place = origin(p)
             for k in range(LIST // 2, LIST):
-                entry(k)
-
-        return _
-
-    lax.fori_loop(0, LIST, slot, 0)
+                enter(p, k, at, count, start, place)
+            return _
+
+        lax.fori_loop(0, LIST, rest, 0)
 
 
 def swap(low, high, is_low, width):
@@ -708,7 +716,7 @@
     lane = place[1:2, :].astype(jnp.int32) + 32
     hot = jnp.where(iota((128, 512), 0) == lane, 1.0, 0.0).astype(BF16)
     total = jnp.zeros((160, 512), F32)
-    for part in split3(found):
+    for part in split3(found)[:2]:
         total = total + jnp.dot(part, hot, preferred_element_type=F32)
     here = (iota((8, 512), 0) == place[0:1, :].astype(jnp.int32)) & (place[2:3, :] > 0.0)
     for k in range(20):

time: 49.3 us -> 49.1 us (level)
  no operation moved by 1% of the time
where the time goes in v8:
time: 49.1 us; the launch traced here: 48.9 us
  Pallas kernels  47.5 us (97%)
  other arithmetic  0.8 us (2%)
  between operations  0.64 us (1%)
    pallas_call x1, Pallas kernels, exchange_call(): pl.pallas_call(exchange, out_shape=(jax.ShapeDtypeStruct((LAYERS, 8, 4, 4...  30 us
    pallas_call x1, Pallas kernels, sweep_call(): pl.pallas_call(sweep, out_shape=(jax.ShapeDtypeStruct((15, 512), F32), ja...  17.4 us

profile of v8, /device:TPU:1, one launch (start us, length us, event | category | flops | bytes accessed | tf_op | source)
XLA Modules:
  0.0 48.9 jit_solution(11444005433018588308)
XLA Ops:
  0.6 0.8 %convert_add_fusion.values = f32[12,512]{1,0:T(8,128)S(1)} fusion(s32[1,2]{1,0:T(1,128)} %bitcast.11, s32[2,14]{1,0:T(2,128)} %bitcast.10, f32[1,512]{1,0:T(1,128)} %bitcast.8, f32[3,512]{1,0:T(4,128)} %param.8, f32[1,512]{1,0:T(1,128)} %bitcast.9, f32[4,512]{1,0:T(4,128)} %param.6), kind=kLoop, calls=%fused_computation | loop fusion | flops 36864 | bytes 43128 | tf_op jit(solution)/shard_map/add | solution.py:202
  1.4 30.0 %gather_sites.1 = (f32[3,8,4,40,128]{4,3,2,1,0:T(8,128)S(1)}, f32[8,512]{1,0:T(8,128)S(1)}, s32[24,128]{1,0:T(8,128)S(1)}) custom-call(f32[12,512]{1,0:T(8,128)S(1)} %convert_add_fusion.values), custom_call_target="tpu_custom_call" | custom-call | tf_op jit(solution)/shard_map/gather_sites/pallas_call | solution.py:204
  31.5 17.4 %sweep.1 = (f32[15,512]{1,0:T(8,128)}, f32[5,512]{1,0:T(8,128)}) custom-call(s32[3072]{0:T(1024)S(1)} %bitcast.7, f32[96,40,128]{2,1,0:T(8,128)S(1)} %bitcast.6, f32[8,512]{1,0:T(8,128)S(1)} %get-tuple-element.7.place), custom_call_target="tpu_custom_call" | custom-call | tf_op jit(solution)/shard_map/sweep/pallas_call | solution.py:733
